TPU v7x, 32 devices: a whole 2x2x4 slice. The times are simulated.
32 devices in a mesh: lon: 8 (over z, y), ch: 4 (over x, core).
Axes of the slice: x: 2, y: 2, z: 4, core: 2. Of those that a mesh axis runs over, the one named last changes fastest.
Arguments:
- ocean_state: bfloat16 [400, 64, 1024], P('ch', None, 'lon'), may hold values from -6 to 6
- sea_mask: int32 [64, 1024], P(None, 'lon'), may hold values 0 or 1
- kernel: float32 [400, 49], P('ch'), may hold values from -0.875 to 0.875
- conv_bias: float32 [400], P('ch'), may hold values from -3 to 3
- norm_gain: float32 [400], replicated, may hold values from 0.1 to 1.9
- norm_bias: float32 [400], replicated, may hold values from -2 to 2
- weight_in: bfloat16 [400, 1600], replicated, may hold values from -0.3125 to 0.3125
- bias_in: float32 [1600], replicated, may hold values from -3 to 3
- weight_out: bfloat16 [1600, 400], replicated, may hold values from -0.15625 to 0.15625
- bias_out: float32 [400], replicated, may hold values from -3 to 3
- layer_scale: float32 [400], P('ch'), may hold values from 0.5 to 2
- cotangent: bfloat16 [400, 64, 1024], P('ch', None, 'lon'), may hold values from -6 to 6
Outputs:
- updated: bfloat16 [400, 64, 1024], P('ch', None, 'lon')
- grad_state: bfloat16 [400, 64, 1024], P('ch', None, 'lon')
- grad_weight_in: float32 [400, 1600], replicated
- grad_weight_out: float32 [1600, 400], replicated
Inputs may be any that keep to these rules, and one draw needn't show every extreme that they name: `sea_mask`: 1 marks an ocean cell, 0 a land cell.
All inputs are finite; a program needn't handle non-finite values. No bound on the sum of `sea_mask` on one device may be relied on, other than what follows from the above.
Results may differ from a plain program's by a relative error of at most 0.0077.
Values may be sent and summed in bfloat16 or wider, within the bound.
A program may use at most 192 MiB of HBM per device.

v0:
```python
import math

import jax
import jax.numpy as jnp
from jax import lax
from jax.sharding import PartitionSpec as P

KW = 7


root_coef = math.sqrt(2.0 / math.pi)
cubic_coef = 0.044715
norm_eps = 1e-06


def extended(cells, sides, width):
    for axis, dim in sides:
        count = lax.axis_size(axis)
        head = lax.slice_in_dim(cells, 0, width, axis=dim)
        tail = lax.slice_in_dim(cells, cells.shape[dim] - width, cells.shape[dim], axis=dim)
        cells = jnp.concatenate(
            [
                lax.ppermute(tail, axis, [(i, (i + 1) % count) for i in range(count)]),
                cells,
                lax.ppermute(head, axis, [((i + 1) % count, i) for i in range(count)]),
            ],
            axis=dim,
        )
    return cells


def gelu_parts(pre_act):
    inner_arg = root_coef * (pre_act + cubic_coef * pre_act * pre_act * pre_act)
    tangent = jnp.tanh(inner_arg)
    gelu_value = 0.5 * pre_act * (1.0 + tangent)
    gelu_slope = 0.5 * (1.0 + tangent) + 0.5 * pre_act * (1.0 - tangent * tangent) * root_coef * (
        1.0 + 3.0 * cubic_coef * pre_act * pre_act
    )
    return (gelu_value, gelu_slope)


def depth_taps(padded, kernel, row_count, lon_cells):
    tap_total = jnp.zeros((padded.shape[0], row_count, lon_cells), jnp.float32)
    for row_off in range(KW):
        for col_off in range(KW):
            tap_total = (
                tap_total
                + kernel[:, row_off * KW + col_off][:, None, None]
                * padded[:, row_off : row_off + row_count, col_off : col_off + lon_cells]
            )
    return tap_total


def depth_back(padded_grad, kernel, row_count, lon_cells):
    span = KW - 1
    tap_total = jnp.zeros((padded_grad.shape[0], row_count, lon_cells), jnp.float32)
    for row_off in range(KW):
        for col_off in range(KW):
            tap_total = (
                tap_total
                + kernel[:, row_off * KW + col_off][:, None, None]
                * padded_grad[
                    :,
                    span - row_off : span - row_off + row_count,
                    span - col_off : span - col_off + lon_cells,
                ]
            )
    return tap_total


def block_math(
    conv_cells, grad_cells, norm_gain, norm_bias, weight_in, bias_in, weight_out, bias_out
):
    full_width = conv_cells.shape[0]
    values = conv_cells.astype(jnp.float32)
    mean_val = jnp.sum(values, axis=0) / full_width
    square = jnp.sum(values * values, axis=0) / full_width
    inv_std = lax.rsqrt(square - mean_val * mean_val + norm_eps)
    centred = (values - mean_val) * inv_std
    normed = (centred * norm_gain[:, None] + norm_bias[:, None]).astype(jnp.bfloat16)
    pre_act = jnp.dot(weight_in.T, normed, preferred_element_type=jnp.float32) + bias_in[:, None]
    gelu_value, gelu_slope = gelu_parts(pre_act)
    activation = gelu_value.astype(jnp.bfloat16)
    branch = (
        jnp.dot(weight_out.T, activation, preferred_element_type=jnp.float32) + bias_out[:, None]
    ).astype(jnp.bfloat16)
    grad_act = jnp.dot(weight_out, grad_cells, preferred_element_type=jnp.float32)
    grad_pre = (grad_act * gelu_slope).astype(jnp.bfloat16)
    part_out = jnp.dot(activation, grad_cells.T, preferred_element_type=jnp.float32)
    part_in = jnp.dot(normed, grad_pre.T, preferred_element_type=jnp.float32)
    grad_normed = jnp.dot(weight_in, grad_pre, preferred_element_type=jnp.float32)
    scaled_grad = grad_normed * norm_gain[:, None]
    mean_first = jnp.sum(scaled_grad, axis=0) / full_width
    mean_second = jnp.sum(scaled_grad * centred, axis=0) / full_width
    grad_conv = (inv_std * (scaled_grad - mean_first - centred * mean_second)).astype(jnp.bfloat16)
    return (branch, grad_conv, part_in, part_out)


def body(
    ocean_state,
    sea_mask,
    kernel,
    conv_bias,
    norm_gain,
    norm_bias,
    weight_in,
    bias_in,
    weight_out,
    bias_out,
    layer_scale,
    cotangent,
):
    local_chan, row_count, lon_cells = ocean_state.shape
    chan_groups = lax.axis_size("ch")
    full_width = local_chan * chan_groups
    rim_width = KW // 2
    grad_scale = 1.0 / math.sqrt(row_count * lon_cells * lax.axis_size("lon"))
    state_f = ocean_state.astype(jnp.float32)
    state_rim = extended(ocean_state, (("lon", 2),), rim_width)
    padded = jnp.pad(state_rim.astype(jnp.float32), ((0, 0), (rim_width, rim_width), (0, 0)))
    conv_out = (depth_taps(padded, kernel, row_count, lon_cells) + conv_bias[:, None, None]).astype(
        jnp.bfloat16
    )
    mask_f = sea_mask.astype(jnp.float32)[None]
    grad_out = cotangent.astype(jnp.float32) * mask_f
    grad_branch = (grad_out * layer_scale[:, None, None]).astype(jnp.bfloat16)
    quarter = row_count // chan_groups
    conv_cells, grad_cells = (
        lax.all_to_all(conv_out, "ch", split_axis=1, concat_axis=0, tiled=True),
        lax.all_to_all(grad_branch, "ch", split_axis=1, concat_axis=0, tiled=True),
    )
    branch_cells, conv_grad_cells, part_in, part_out = block_math(
        conv_cells.reshape(full_width, quarter * lon_cells),
        grad_cells.reshape(full_width, quarter * lon_cells),
        norm_gain,
        norm_bias,
        weight_in,
        bias_in,
        weight_out,
        bias_out,
    )
    branch, grad_conv = (
        lax.all_to_all(
            branch_cells.reshape(full_width, quarter, lon_cells),
            "ch",
            split_axis=0,
            concat_axis=1,
            tiled=True,
        ),
        lax.all_to_all(
            conv_grad_cells.reshape(full_width, quarter, lon_cells),
            "ch",
            split_axis=0,
            concat_axis=1,
            tiled=True,
        ),
    )
    sum_in, sum_out = lax.psum((part_in, part_out), ("lon", "ch"))
    grad_weight_in = sum_in * grad_scale
    grad_weight_out = sum_out * grad_scale
    updated = (mask_f * (state_f + layer_scale[:, None, None] * branch.astype(jnp.float32))).astype(
        jnp.bfloat16
    )
    grad_rim = extended(grad_conv, (("lon", 2),), rim_width)
    padded_grad = jnp.pad(grad_rim.astype(jnp.float32), ((0, 0), (rim_width, rim_width), (0, 0)))
    grad_state = (grad_out + depth_back(padded_grad, kernel, row_count, lon_cells)).astype(
        jnp.bfloat16
    )
    return (updated, grad_state, grad_weight_in, grad_weight_out)


def solution(mesh):
    return jax.shard_map(
        body,
        mesh=mesh,
        in_specs=(
            P("ch", None, "lon"),
            P(None, "lon"),
            P("ch", None),
            P("ch"),
            P(),
            P(),
            P(),
            P(),
            P(),
            P(),
            P("ch"),
            P("ch", None, "lon"),
        ),
        out_specs=(P("ch", None, "lon"), P("ch", None, "lon"), P(), P()),
        check_vma=False,
    )
```

profile of v0, /device:TPU:0, one launch (start us, length us, event | category | flops | bytes accessed | tf_op | source)
XLA Modules:
  0.0 402.8 jit_solution(13743698533383384451)
XLA Ops:
  7.2 4.5 %fusion.192 = (bf16[100,64,3]{2,1,0:T(8,128)(2,1)}, bf16[100,64,3]{2,1,0:T(8,128)(2,1)}) fusion(bf16[100,64,128]{2,1,0:T(8,128)(2,1)} %param.12), kind=kLoop, calls=%fused_computation.345 | loop fusion | bytes 153600 | tf_op jit(solution)/shard_map/slice | solution.py:20
  11.7 2.9 copy.40
  14.6 3.0 collective-permute-start
  17.6 2.9 copy.41
  20.5 3.1 collective-permute-start.1
  24.3 2.2 copy.23
  30.2 4.3 %maximum_convert_fusion = f32[100,64,134]{2,0,1:T(8,128)S(1)} fusion(bf16[100,64,3]{2,0,1:T(8,128)(2,1)} %copy.28, bf16[100,64,128]{2,0,1:T(8,128)(2,1)} %copy.23, bf16[100,64,3]{2,0,1:T(8,128)(2,1)} %copy.26), kind=kLoop, calls=%fused_computation.82 | loop fusion | flops 5145600 | bytes 5145600 | tf_op jit(solution)/shard_map/convert_element_type | solution.py:120
  34.5 40.2 %add_convert_fusion = bf16[100,64,128]{2,0,1:T(8,128)(2,1)} fusion(f32[100,64,134]{2,0,1:T(8,128)S(1)} %maximum_convert_fusion, f32[100]{0:T(128)} %param.15, f32[100]{0:T(128)} %get-tuple-element.66, f32[100]{0:T(128)} %get-tuple-element.67, f32[100]{0:T(128)S(1)} %get-tuple-element.20, f32[100]{0:T(128)S(1)} %get-tuple-element.21, ...), kind=kLoop, calls=%fused_computation.176 | loop fusion | flops 81100800 | bytes 32333840 | tf_op jit(solution)/shard_map/convert_element_type | solution.py:121
  74.7 25.3 %all_to_all.51 = bf16[100,64,128]{2,0,1:T(8,128)(2,1)S(1)} all-to-all(bf16[100,64,128]{2,0,1:T(8,128)(2,1)} %add_convert_fusion), channel_id=1, replica_groups=mesh['lon'=8,'ch'=4] {'ch'}, dimensions={1} | all-to-all | bytes 3276800 | tf_op jit(solution)/shard_map/all_to_all | solution.py:129
  100.6 10.9 %multiply_convert_fusion = (bf16[1600,2048]{1,0:T(8,128)(2,1)S(1)}, f32[2048,1600]{0,1:T(8,128)}) fusion(f32[1600]{0:T(1024)S(1)} %copy-done.23, bf16[400,1600]{1,0:T(8,128)(2,1)S(1)} %copy-done, f32[50,8,16,128]{3,2,1,0:T(8,128)S(1)} %bitcast.202, f32[400]{0:T(512)S(1)} %copy-done.25, f32[400]{0:T(512)S(1)} %copy-done.26, f32[2048]{0:T(1024)S(1)} %fusion.188, ...), kind=kOutput, calls=%fused_computation.10 | convolution fusion | flops 2658304000 | bytes 24243584 | tf_op jit(solution)/shard_map/dot_general | solution.py:81
  111.6 3.2 fusion.184
  116.4 4.5 %all-to-all-start.1 = ((bf16[400,16,128]{2,1,0:T(8,128)(2,1)}), bf16[400,16,128]{2,1,0:T(8,128)(2,1)}, u32[]{:S(2)}, u32[]{:S(2)}) async-start(bf16[400,16,128]{2,1,0:T(8,128)(2,1)} %bitcast.209), calls=%async_computation.1 | async-start | bytes 3276800 | tf_op jit(solution)/shard_map/all_to_all | solution.py:143
  121.0 20.8 %all-to-all-done.1 = bf16[400,16,128]{2,1,0:T(8,128)(2,1)} async-done(((bf16[400,16,128]{2,1,0:T(8,128)(2,1)}), bf16[400,16,128]{2,1,0:T(8,128)(2,1)}, u32[]{:S(2)}, u32[]{:S(2)}) %all-to-all-start.1) | async-done | bytes 1638432 | tf_op jit(solution)/shard_map/all_to_all | solution.py:143
  141.8 1.9 copy.30
  143.7 3.6 multiply_convert_fusion.1
  147.3 24.3 %all_to_all.52 = bf16[100,64,128]{2,0,1:T(8,128)(2,1)S(1)} all-to-all(bf16[100,64,128]{2,0,1:T(8,128)(2,1)S(1)} %get-tuple-element.17), channel_id=1, replica_groups=mesh['lon'=8,'ch'=4] {'ch'}, dimensions={1} | all-to-all | bytes 3276800 | tf_op jit(solution)/shard_map/all_to_all | solution.py:130
  171.8 14.4 %fusion.6 = bf16[1600,2048]{1,0:T(8,128)(2,1)S(1)} fusion(f32[2048,1600]{0,1:T(8,128)} %get-tuple-element.69, bf16[1600,400]{0,1:T(8,128)(2,1)S(1)} %copy-done.22, f32[1600]{0:T(1024)S(1)} %copy-done.23, bf16[50,8,16,128]{3,2,1,0:T(8,128)(2,1)S(1)} %bitcast.210), kind=kOutput, calls=%fused_computation.8 | convolution fusion | flops 2686976000 | bytes 22585600 | tf_op jit(solution)/shard_map/dot_general | solution.py:87
  186.2 5.6 %fusion.178 = (f32[2048]{0:T(1024)S(1)}, f32[2048,400]{0,1:T(8,128)}) fusion(f32[50,8,16,128]{3,2,1,0:T(8,128)S(1)} %bitcast.205, f32[2048]{0:T(1024)S(1)} %fusion.188, f32[2048]{0:T(1024)S(1)} %multiply_bitcast_fusion, f32[400]{0:T(512)S(1)} %copy-done.26, bf16[400,1600]{1,0:T(8,128)(2,1)S(1)} %copy-done, bf16[1600,2048]{1,0:T(8,128)(2,1)S(1)} %fusion.6), kind=kOutput, calls=%fused_computation.271 | convolution fusion | flops 2625533952 | bytes 14413376 | tf_op jit(solution)/shard_map/dot_general | solution.py:91
  191.8 2.1 reduce_sum.38
  193.9 4.8 %fusion.180 = bf16[50,8,16,128]{3,1,2,0:T(8,128)(2,1)S(1)} fusion(f32[50,8,16,128]{3,2,1,0:T(8,128)} %bitcast.203, f32[2048,400]{0,1:T(8,128)} %get-tuple-element.71, f32[2048]{0:T(1024)S(1)} %get-tuple-element.72, f32[2048]{0:T(1024)S(1)} %get-tuple-element.73, f32[2048]{0:T(1024)S(1)} %fusion.188, f32[2048]{0:T(1024)S(1)} %multiply_bitcast_fusion), kind=kLoop, calls=%fused_computation.278 | loop fusion | flops 5734400 | bytes 8224768
  200.3 4.4 %all-to-all-start.3 = ((bf16[400,16,128]{2,1,0:T(8,128)(2,1)}), bf16[400,16,128]{2,1,0:T(8,128)(2,1)}, u32[]{:S(2)}, u32[]{:S(2)}) async-start(bf16[400,16,128]{2,1,0:T(8,128)(2,1)} %bitcast.208), calls=%async_computation.3 | async-start | bytes 3276800 | tf_op jit(solution)/shard_map/all_to_all | solution.py:150
  206.4 9.2 %fusion.189 = f32[400,1600]{1,0:T(8,128)} fusion(bf16[1600,2048]{1,0:T(8,128)(2,1)} %copy-done.27, f32[50,8,16,128]{3,2,1,0:T(8,128)} %bitcast.204, f32[400]{0:T(512)S(1)} %copy-done.25, f32[400]{0:T(512)S(1)} %copy-done.26, f32[2048]{0:T(1024)S(1)} %fusion.188, f32[2048]{0:T(1024)S(1)} %multiply_bitcast_fusion), kind=kOutput, calls=%fused_computation.342 | convolution fusion | flops 2625536000 | bytes 12409984 | tf_op jit(solution)/shard_map/dot_general | solution.py:90
  215.6 10.0 %all-to-all-done.3 = bf16[400,16,128]{2,1,0:T(8,128)(2,1)} async-done(((bf16[400,16,128]{2,1,0:T(8,128)(2,1)}), bf16[400,16,128]{2,1,0:T(8,128)(2,1)}, u32[]{:S(2)}, u32[]{:S(2)}) %all-to-all-start.3) | async-done | bytes 1638432 | tf_op jit(solution)/shard_map/all_to_all | solution.py:150
  229.2 1.9 copy.34
  232.1 5.0 %collective-permute-start.3 = (bf16[100,64,3]{0,1,2:T(8,128)(2,1)S(1)}, bf16[100,64,3]{0,1,2:T(8,128)(2,1)S(1)}, u32[]{:S(2)}, u32[]{:S(2)}) collective-permute-start(bf16[100,64,3]{0,1,2:T(8,128)(2,1)S(1)} %copy.35), channel_id=1, source_target_pairs={{4,0},{8,4},{12,8},{16,12},{20,16},{24,20},{28,24},{0,28},{5,1},{9... | collective-permute-start | bytes 115208 | tf_op jit(solution)/shard_map/ppermute | solution.py:25
  237.1 8.0 %fusion.181 = f32[1600,400]{0,1:T(8,128)} fusion(bf16[1600,2048]{1,0:T(8,128)(2,1)} %copy-done.28, bf16[50,8,16,128]{3,2,1,0:T(8,128)(2,1)} %bitcast.211), kind=kOutput, calls=%fused_computation.279 | convolution fusion | flops 2621440000 | bytes 10752000 | tf_op jit(solution)/shard_map/dot_general | solution.py:89
  247.0 1.9 copy.37
  248.8 4.3 %maximum_convert_fusion.1 = f32[100,64,134]{2,0,1:T(8,128)S(1)} fusion(bf16[100,64,3]{2,0,1:T(8,128)(2,1)} %copy.37, bf16[100,64,128]{2,0,1:T(8,128)(2,1)} %bitcast.201, bf16[100,64,3]{2,0,1:T(8,128)(2,1)} %copy.36), kind=kLoop, calls=%fused_computation.83 | loop fusion | flops 5145600 | bytes 5145600 | tf_op jit(solution)/shard_map/convert_element_type | solution.py:165
  253.1 41.0 %fusion.173 = bf16[100,64,128]{2,0,1:T(8,128)(2,1)} fusion(f32[100,64,134]{2,0,1:T(8,128)S(1)} %maximum_convert_fusion.1, f32[100]{0:T(128)} %get-tuple-element.66, f32[100]{0:T(128)} %get-tuple-element.67, f32[100]{0:T(128)S(1)} %get-tuple-element.20, f32[100]{0:T(128)S(1)} %get-tuple-element.21, f32[100]{0:T(128)S(1)} %get-tuple-element.22, ...), kind=kLoop, calls=%fused_computation.263 | loop fusion | flops 82739200 | bytes 34003712 | tf_op jit(solution)/shard_map/convert_element_type | solution.py:166
  294.2 3.1 copy.39
  297.2 93.1 %all-reduce.5.cloned.1.call-done = (f32[400,1600]{1,0:T(8,128)}, f32[1600,400]{0,1:T(8,128)}) async-done(((f32[400,1600]{1,0:T(8,128)}, f32[1600,400]{0,1:T(8,128)}), (f32[400,1600]{1,0:T(8,128)}, f32[1600,400]{0,1:T(8,128)})) %all-reduce.5.cloned.1.call-update) | async-done | bytes 5120016 | tf_op jit(solution)/shard_map/psum | solution.py:158
  390.3 3.6 broadcast_multiply_fusion
  (84 shorter events, 18.1 us)
Async XLA Ops:
  7.2 93.4 %copy-start = (bf16[400,1600]{1,0:T(8,128)(2,1)S(1)}, bf16[400,1600]{1,0:T(8,128)(2,1)}, u32[]{:S(2)}) copy-start(bf16[400,1600]{1,0:T(8,128)(2,1)} %param.18) | copy-start | bytes 3840004
  7.2 17.1 %copy-start.2 = (bf16[100,64,128]{2,1,0:T(8,128)(2,1)S(1)}, bf16[100,64,128]{2,1,0:T(8,128)(2,1)}, u32[]{:S(2)}) copy-start(bf16[100,64,128]{2,1,0:T(8,128)(2,1)} %param.12) | copy-start | bytes 4915204
  7.2 16.4 %copy-start.11 = (f32[100,49]{0,1:T(8,128)S(1)}, f32[100,49]{0,1:T(8,128)}, u32[]{:S(2)}) copy-start(f32[100,49]{0,1:T(8,128)} %param.14) | copy-start | bytes 58804
  14.6 12.0 %collective-permute-start = (bf16[100,64,3]{0,1,2:T(8,128)(2,1)S(1)}, bf16[100,64,3]{0,1,2:T(8,128)(2,1)S(1)}, u32[]{:S(2)}, u32[]{:S(2)}) collective-permute-start(bf16[100,64,3]{0,1,2:T(8,128)(2,1)S(1)} %copy.40), channel_id=1, source_target_pairs={{0,4},{4,8},{8,12},{12,16},{16,20},{20,24},{24,28},{28,0},{1,5},{5... | collective-permute-start | bytes 115208 | tf_op jit(solution)/shard_map/ppermute | solution.py:23
  20.5 7.9 %collective-permute-start.1 = (bf16[100,64,3]{0,1,2:T(8,128)(2,1)S(1)}, bf16[100,64,3]{0,1,2:T(8,128)(2,1)S(1)}, u32[]{:S(2)}, u32[]{:S(2)}) collective-permute-start(bf16[100,64,3]{0,1,2:T(8,128)(2,1)S(1)} %copy.41), channel_id=1, source_target_pairs={{4,0},{8,4},{12,8},{16,12},{20,16},{24,20},{28,24},{0,28},{5,1},{9... | collective-permute-start | bytes 115208 | tf_op jit(solution)/shard_map/ppermute | solution.py:25
  23.6 10.8 %copy-start.12 = (f32[100]{0:T(128)}, f32[100]{0:T(128)S(1)}, u32[]{:S(2)}) copy-start(f32[100]{0:T(128)S(1)} %get-tuple-element.52) | copy-start | bytes 1204
  23.6 10.8 %copy-start.13 = (f32[100]{0:T(128)}, f32[100]{0:T(128)S(1)}, u32[]{:S(2)}) copy-start(f32[100]{0:T(128)S(1)} %get-tuple-element.53) | copy-start | bytes 1204
  23.7 10.8 %copy-start.14 = (f32[100]{0:T(128)}, f32[100]{0:T(128)S(1)}, u32[]{:S(2)}) copy-start(f32[100]{0:T(128)S(1)} %get-tuple-element.54) | copy-start | bytes 1204
  23.7 10.8 %copy-start.15 = (f32[100]{0:T(128)}, f32[100]{0:T(128)S(1)}, u32[]{:S(2)}) copy-start(f32[100]{0:T(128)S(1)} %get-tuple-element.55) | copy-start | bytes 1204
  23.7 10.8 %copy-start.16 = (f32[100]{0:T(128)}, f32[100]{0:T(128)S(1)}, u32[]{:S(2)}) copy-start(f32[100]{0:T(128)S(1)} %get-tuple-element.56) | copy-start | bytes 1204
  24.3 10.2 %copy-start.17 = (f32[100]{0:T(128)}, f32[100]{0:T(128)S(1)}, u32[]{:S(2)}) copy-start(f32[100]{0:T(128)S(1)} %get-tuple-element.57) | copy-start | bytes 1204
  24.3 10.2 %copy-start.18 = (f32[100]{0:T(128)}, f32[100]{0:T(128)S(1)}, u32[]{:S(2)}) copy-start(f32[100]{0:T(128)S(1)} %get-tuple-element.58) | copy-start | bytes 1204
  24.3 10.2 %copy-start.19 = (f32[100]{0:T(128)}, f32[100]{0:T(128)S(1)}, u32[]{:S(2)}) copy-start(f32[100]{0:T(128)S(1)} %get-tuple-element.59) | copy-start | bytes 1204
  74.7 25.9 %copy-start.23 = (f32[1600]{0:T(1024)S(1)}, f32[1600]{0:T(1024)}, u32[]{:S(2)}) copy-start(f32[1600]{0:T(1024)} %param.19) | copy-start | bytes 19204
  74.7 25.9 %copy-start.25 = (f32[400]{0:T(512)S(1)}, f32[400]{0:T(512)}, u32[]{:S(2)}) copy-start(f32[400]{0:T(512)} %param.17) | copy-start | bytes 4804
  74.7 25.9 %copy-start.26 = (f32[400]{0:T(512)S(1)}, f32[400]{0:T(512)}, u32[]{:S(2)}) copy-start(f32[400]{0:T(512)} %param.16) | copy-start | bytes 4804
  100.5 11.0 %copy-start.4 = (f32[100,4,16,128]{3,2,0,1:T(8,128)}, f32[100,4,16,128]{3,2,0,1:T(8,128)S(1)}, u32[]{:S(2)}) copy-start(f32[100,4,16,128]{3,2,0,1:T(8,128)S(1)} %get-tuple-element.12) | copy-start | bytes 9830404
  100.6 11.0 %copy-start.21 = (bf16[1600,400]{0,1:T(8,128)(2,1)S(1)}, bf16[1600,400]{0,1:T(8,128)(2,1)}, u32[]{:S(2)}) copy-start(bf16[1600,400]{0,1:T(8,128)(2,1)} %param.20) | copy-start | bytes 3840004
  100.6 11.0 %copy-start.24 = (f32[400]{0:T(512)S(1)}, f32[400]{0:T(512)}, u32[]{:S(2)}) copy-start(f32[400]{0:T(512)} %param.21) | copy-start | bytes 4804
  114.8 6.1 %copy-start.10 = (s32[64,128]{1,0:T(8,128)S(1)}, s32[64,128]{1,0:T(8,128)}, u32[]{:S(2)}) copy-start(s32[64,128]{1,0:T(8,128)} %param.13) | copy-start | bytes 98308
  116.4 27.2 %copy-start.3 = (bf16[100,64,128]{2,1,0:T(8,128)(2,1)S(1)}, bf16[100,64,128]{2,1,0:T(8,128)(2,1)}, u32[]{:S(2)}) copy-start(bf16[100,64,128]{2,1,0:T(8,128)(2,1)} %param.12) | copy-start | bytes 4915204
  116.4 27.2 %copy-start.20 = (f32[100]{0:T(128)S(1)}, f32[100]{0:T(128)}, u32[]{:S(2)}) copy-start(f32[100]{0:T(128)} %param.22) | copy-start | bytes 1204
  116.4 25.3 %all-to-all-start.1 = ((bf16[400,16,128]{2,1,0:T(8,128)(2,1)}), bf16[400,16,128]{2,1,0:T(8,128)(2,1)}, u32[]{:S(2)}, u32[]{:S(2)}) async-start(bf16[400,16,128]{2,1,0:T(8,128)(2,1)} %bitcast.209), calls=%async_computation.1 | async-start | bytes 3276800 | tf_op jit(solution)/shard_map/all_to_all | solution.py:143
  147.3 24.5 %copy-start.22 = (bf16[1600,400]{0,1:T(8,128)(2,1)S(1)}, bf16[1600,400]{0,1:T(8,128)(2,1)}, u32[]{:S(2)}) copy-start(bf16[1600,400]{0,1:T(8,128)(2,1)} %param.20) | copy-start | bytes 3840004
  171.8 14.4 %copy-start.9 = (bf16[100,4,16,128]{3,2,0,1:T(8,128)(2,1)}, bf16[100,4,16,128]{3,2,0,1:T(8,128)(2,1)S(1)}, u32[]{:S(2)}) copy-start(bf16[100,4,16,128]{3,2,0,1:T(8,128)(2,1)S(1)} %copy.32) | copy-start | bytes 4915204
  171.8 14.4 %copy-start.5 = (f32[100,4,16,128]{3,2,0,1:T(8,128)S(1)}, f32[100,4,16,128]{3,2,0,1:T(8,128)}, u32[]{:S(2)}) copy-start(f32[100,4,16,128]{3,2,0,1:T(8,128)} %copy-done.4) | copy-start | bytes 9830404
  186.2 5.6 %copy-start.27 = (bf16[1600,2048]{1,0:T(8,128)(2,1)}, bf16[1600,2048]{1,0:T(8,128)(2,1)S(1)}, u32[]{:S(2)}) copy-start(bf16[1600,2048]{1,0:T(8,128)(2,1)S(1)} %fusion.6) | copy-start | bytes 19660804
  198.7 6.0 %copy-start.6 = (bf16[100,64,128]{2,0,1:T(8,128)(2,1)S(1)}, bf16[100,64,128]{2,0,1:T(8,128)(2,1)}, u32[]{:S(2)}) copy-start(bf16[100,64,128]{2,0,1:T(8,128)(2,1)} %get-tuple-element.18) | copy-start | bytes 4915204
  200.3 25.2 %all-to-all-start.3 = ((bf16[400,16,128]{2,1,0:T(8,128)(2,1)}), bf16[400,16,128]{2,1,0:T(8,128)(2,1)}, u32[]{:S(2)}, u32[]{:S(2)}) async-start(bf16[400,16,128]{2,1,0:T(8,128)(2,1)} %bitcast.208), calls=%async_computation.3 | async-start | bytes 3276800 | tf_op jit(solution)/shard_map/all_to_all | solution.py:150
  204.7 185.6 %all-reduce.5.cloned.1.call-start = ((), (), s32[]{:S(2)}) async-start(), calls=%async_computation.4 | async-start | bytes 10649600 | tf_op jit(solution)/shard_map/psum | solution.py:158
  231.2 14.0 %collective-permute-start.2 = (bf16[100,64,3]{0,1,2:T(8,128)(2,1)S(1)}, bf16[100,64,3]{0,1,2:T(8,128)(2,1)S(1)}, u32[]{:S(2)}, u32[]{:S(2)}) collective-permute-start(bf16[100,64,3]{0,1,2:T(8,128)(2,1)S(1)} %copy.34), channel_id=1, source_target_pairs={{0,4},{4,8},{8,12},{12,16},{16,20},{20,24},{24,28},{28,0},{1,5},{5... | collective-permute-start | bytes 115208 | tf_op jit(solution)/shard_map/ppermute | solution.py:23
  232.1 14.8 %collective-permute-start.3 = (bf16[100,64,3]{0,1,2:T(8,128)(2,1)S(1)}, bf16[100,64,3]{0,1,2:T(8,128)(2,1)S(1)}, u32[]{:S(2)}, u32[]{:S(2)}) collective-permute-start(bf16[100,64,3]{0,1,2:T(8,128)(2,1)S(1)} %copy.35), channel_id=1, source_target_pairs={{4,0},{8,4},{12,8},{16,12},{20,16},{24,20},{28,24},{0,28},{5,1},{9... | collective-permute-start | bytes 115208 | tf_op jit(solution)/shard_map/ppermute | solution.py:25
  (4 other events, 10.6 us)
Sparse Core Ops, SparseCore 0:
  245.3 144.9 all-reduce.4
where the time goes:
time: 410 us; the launch traced here: 403 us
  waiting for transfers between devices  124 us (30%)
  other arithmetic  106 us (26%)
  matrix products  51.3 us (13%)
  blocking collectives  49.6 us (12%)
  local copies, waits for them, and re-layouts  37 us (9%)
  starting transfers between devices  20.1 us (5%)
  between operations  14.9 us (4%)
    psum x1, waiting for transfers between devices, body(): sum_in, sum_out = lax.psum((part_in, part_out), ('lon', 'ch'))  93.1 us
    convert_element_type x1, other arithmetic, body(): (grad_out + depth_back(padded_grad, kernel, row_count, lon_cells)).astype...  41 us
    convert_element_type x1, other arithmetic, body(): (depth_taps(padded, kernel, row_count, lon_cells) + conv_bias[:, None, No...  40.2 us
    all_to_all x1, blocking collectives, body(): lax.all_to_all(conv_out, 'ch', split_axis=1, concat_axis=0, tiled=True)  25.3 us
    all_to_all x1, blocking collectives, body(): lax.all_to_all(grad_branch, 'ch', split_axis=1, concat_axis=0, tiled=True)  24.3 us
    all_to_all x1, waiting for transfers between devices, body(): lax.all_to_all(branch_cells.reshape(full_width, quarter, lon_cells), 'ch'...  20.8 us
    unnamed x65, local copies, waits for them, and re-layouts  16 us
    dot_general x1, matrix products, block_math(): jnp.dot(weight_out, grad_cells, preferred_element_type=jnp.float32)  14.4 us
  transfers between devices with their start and end apart: 7, of which 3 were waited for; matrix products, arithmetic and copies ran while one was open for 20% of the time, Pallas kernels for 0%

commit v1 on v0

v1 whole, which is shorter than its diff:
```python
import functools
import math

import jax
import jax.numpy as jnp
from jax import lax
from jax.experimental import pallas as pl
from jax.experimental.pallas import tpu as pltpu
from jax.sharding import PartitionSpec as P

KW = 7
RIM = KW // 2

root_coef = math.sqrt(2.0 / math.pi)
cubic_coef = 0.044715
norm_eps = 1e-06
VMEM_LIMIT = 56 * 1024 * 1024


def largest_divisor(n, bound):
    return max(d for d in range(1, bound + 1) if n % d == 0)


def rim_exchange(cells):
    count = lax.axis_size("lon")
    width = cells.shape[2]
    head = cells[:, :, :RIM]
    tail = cells[:, :, width - RIM :]
    left = lax.ppermute(tail, "lon", [(i, (i + 1) % count) for i in range(count)])
    right = lax.ppermute(head, "lon", [((i + 1) % count, i) for i in range(count)])
    gap = jnp.zeros(cells.shape[:2] + (width - 2 * RIM,), cells.dtype)
    return jnp.concatenate([right, gap, left], axis=2)


def tap_rows(kernel, row_count):
    taps = kernel.reshape(kernel.shape[0], KW, KW)
    return jnp.repeat(taps, row_count, axis=2)


def conv_channel(cells, rim, taps):
    row_count, width = cells.shape
    cells = cells.astype(jnp.float32)
    rim = rim.astype(jnp.float32)
    lane = lax.broadcasted_iota(jnp.int32, cells.shape, 1)
    shifted = []
    for b in range(KW):
        s = b - RIM
        if s == 0:
            moved = cells
        elif s > 0:
            moved = pltpu.roll(jnp.where(lane < s, rim, cells), width - s, 1)
        else:
            moved = pltpu.roll(jnp.where(lane >= width + s, rim, cells), -s, 1)
        shifted.append(moved.astype(jnp.bfloat16))
    shape = (row_count, KW * row_count)
    offset = (
        lax.rem(lax.broadcasted_iota(jnp.int32, shape, 1), row_count)
        - lax.broadcasted_iota(jnp.int32, shape, 0)
        + RIM
    )
    band = jnp.zeros(shape, jnp.float32)
    for a in range(KW):
        band = jnp.where(offset == a, taps[a : a + 1, :], band)
    return jnp.dot(
        band.astype(jnp.bfloat16),
        jnp.concatenate(shifted, axis=0),
        preferred_element_type=jnp.float32,
    )


def forward_kernel(block, state, rim, cot, mask, taps, bias, scale, conv_out, grad_branch):
    first = pl.program_id(0) * block
    mask_f = mask[...].astype(jnp.float32)

    def channel(k, carry):
        conv = conv_channel(state[k], rim[k], taps[k])
        conv_out[k] = (conv + bias[first + k]).astype(jnp.bfloat16)
        grad_out = cot[k].astype(jnp.float32) * mask_f
        grad_branch[k] = (grad_out * scale[first + k]).astype(jnp.bfloat16)
        return carry

    lax.fori_loop(0, block, channel, 0, unroll=2)


def backward_kernel(
    block, state, branch, grad_conv, rim, cot, mask, taps, scale, updated, grad_state
):
    first = pl.program_id(0) * block
    mask_f = mask[...].astype(jnp.float32)

    def channel(k, carry):
        conv = conv_channel(grad_conv[k], rim[k], taps[k])
        grad_out = cot[k].astype(jnp.float32) * mask_f
        grad_state[k] = (grad_out + conv).astype(jnp.bfloat16)
        value = state[k].astype(jnp.float32) + scale[first + k] * branch[k].astype(jnp.float32)
        updated[k] = (mask_f * value).astype(jnp.bfloat16)
        return carry

    lax.fori_loop(0, block, channel, 0, unroll=2)


def math_kernel(
    hid_block,
    conv_cells,
    grad_cells,
    gain,
    shift,
    win,
    win_t,
    bias_in,
    wout,
    wout_t,
    bias_out,
    branch,
    grad_conv,
    part_in,
    part_out,
    act,
    grad_pre,
):
    @pl.when(pl.program_id(0) == 0)
    def _():
        part_in[...] = jnp.zeros_like(part_in)
        part_out[...] = jnp.zeros_like(part_out)

    full_width = conv_cells.shape[0]
    values = conv_cells[...].astype(jnp.float32)
    mean_val = jnp.sum(values, axis=0, keepdims=True) / full_width
    square = jnp.sum(values * values, axis=0, keepdims=True) / full_width
    inv_std = lax.rsqrt(square - mean_val * mean_val + norm_eps)
    centred = (values - mean_val) * inv_std
    normed = (centred * gain[...] + shift[...]).astype(jnp.bfloat16)
    grads = grad_cells[...]
    across = (((1,), (1,)), ((), ()))
    for start in range(0, win_t.shape[0], hid_block):
        here = slice(start, start + hid_block)
        v = jnp.dot(win_t[here, :], normed, preferred_element_type=jnp.float32) + bias_in[here, :]
        tangent = jnp.tanh(root_coef * (v + cubic_coef * v * v * v))
        act_h = (0.5 * v * (1.0 + tangent)).astype(jnp.bfloat16)
        slope = 0.5 * (1.0 + tangent) + 0.5 * v * (1.0 - tangent * tangent) * root_coef * (
            1.0 + 3.0 * cubic_coef * v * v
        )
        grad_act = jnp.dot(wout[here, :], grads, preferred_element_type=jnp.float32)
        grad_h = (grad_act * slope).astype(jnp.bfloat16)
        act[here, :] = act_h
        grad_pre[here, :] = grad_h
        part_out[here, :] += lax.dot_general(
            act_h, grads, across, preferred_element_type=jnp.float32
        )
        part_in[here, :] += lax.dot_general(
            grad_h, normed, across, preferred_element_type=jnp.float32
        )
    branch[...] = (
        jnp.dot(wout_t[...], act[...], preferred_element_type=jnp.float32) + bias_out[...]
    ).astype(jnp.bfloat16)
    grad_normed = jnp.dot(win[...], grad_pre[...], preferred_element_type=jnp.float32)
    scaled_grad = grad_normed * gain[...]
    mean_first = jnp.sum(scaled_grad, axis=0, keepdims=True) / full_width
    mean_second = jnp.sum(scaled_grad * centred, axis=0, keepdims=True) / full_width
    grad_conv[...] = (inv_std * (scaled_grad - mean_first - centred * mean_second)).astype(
        jnp.bfloat16
    )


def block_math(conv_cells, grad_cells, gain, shift, win, bias_in, wout, bias_out):
    full_width, cells = conv_cells.shape
    hid = win.shape[1]
    block = largest_divisor(cells // 128, 2) * 128
    hid_block = 16 * largest_divisor(hid // 16, 20)
    tile = pl.BlockSpec((full_width, block), lambda i: (0, i))
    whole = lambda shape: pl.BlockSpec(shape, lambda i: (0, 0))
    bf16 = jnp.bfloat16
    part = jax.ShapeDtypeStruct((hid, full_width), jnp.float32)
    return pl.pallas_call(
        functools.partial(math_kernel, hid_block),
        grid=(cells // block,),
        in_specs=[
            tile,
            tile,
            whole((full_width, 1)),
            whole((full_width, 1)),
            whole((full_width, hid)),
            whole((hid, full_width)),
            whole((hid, 1)),
            whole((hid, full_width)),
            whole((full_width, hid)),
            whole((full_width, 1)),
        ],
        out_specs=[tile, tile, whole((hid, full_width)), whole((hid, full_width))],
        out_shape=[
            jax.ShapeDtypeStruct((full_width, cells), bf16),
            jax.ShapeDtypeStruct((full_width, cells), bf16),
            part,
            part,
        ],
        scratch_shapes=[pltpu.VMEM((hid, block), bf16), pltpu.VMEM((hid, block), bf16)],
        compiler_params=pltpu.CompilerParams(vmem_limit_bytes=VMEM_LIMIT),
        name="block_math",
    )(
        conv_cells,
        grad_cells,
        gain[:, None],
        shift[:, None],
        win,
        win.T,
        bias_in[:, None],
        wout,
        wout.T,
        bias_out[:, None],
    )


def body(
    ocean_state,
    sea_mask,
    kernel,
    conv_bias,
    norm_gain,
    norm_bias,
    weight_in,
    bias_in,
    weight_out,
    bias_out,
    layer_scale,
    cotangent,
):
    local_chan, row_count, lon_cells = ocean_state.shape
    chan_groups = lax.axis_size("ch")
    full_width = local_chan * chan_groups
    grad_scale = 1.0 / math.sqrt(row_count * lon_cells * lax.axis_size("lon"))
    block = largest_divisor(local_chan, 10)
    maps = pl.BlockSpec((block, row_count, lon_cells), lambda i: (i, 0, 0))
    one = pl.BlockSpec((row_count, lon_cells), lambda i: (0, 0))
    rows = pl.BlockSpec((block, KW, KW * row_count), lambda i: (i, 0, 0))
    scalars = pl.BlockSpec(memory_space=pltpu.SMEM)
    like = jax.ShapeDtypeStruct(ocean_state.shape, jnp.bfloat16)
    params = pltpu.CompilerParams(vmem_limit_bytes=VMEM_LIMIT)

    conv_out, grad_branch = pl.pallas_call(
        functools.partial(forward_kernel, block),
        grid=(local_chan // block,),
        in_specs=[maps, maps, maps, one, rows, scalars, scalars],
        out_specs=[maps, maps],
        out_shape=[like, like],
        compiler_params=params,
        name="forward_conv",
    )(
        ocean_state,
        rim_exchange(ocean_state),
        cotangent,
        sea_mask,
        tap_rows(kernel, row_count),
        conv_bias,
        layer_scale,
    )
    quarter = row_count // chan_groups
    conv_cells, grad_cells = (
        lax.all_to_all(conv_out, "ch", split_axis=1, concat_axis=0, tiled=True),
        lax.all_to_all(grad_branch, "ch", split_axis=1, concat_axis=0, tiled=True),
    )
    branch_cells, conv_grad_cells, part_in, part_out = block_math(
        conv_cells.reshape(full_width, quarter * lon_cells),
        grad_cells.reshape(full_width, quarter * lon_cells),
        norm_gain,
        norm_bias,
        weight_in,
        bias_in,
        weight_out,
        bias_out,
    )
    sum_in, sum_out = lax.psum((part_in, part_out), ("lon", "ch"))
    branch, grad_conv = (
        lax.all_to_all(
            cells.reshape(full_width, quarter, lon_cells),
            "ch",
            split_axis=0,
            concat_axis=1,
            tiled=True,
        )
        for cells in (branch_cells, conv_grad_cells)
    )
    updated, grad_state = pl.pallas_call(
        functools.partial(backward_kernel, block),
        grid=(local_chan // block,),
        in_specs=[maps, maps, maps, maps, maps, one, rows, scalars],
        out_specs=[maps, maps],
        out_shape=[like, like],
        compiler_params=params,
        name="backward_conv",
    )(
        ocean_state,
        branch,
        grad_conv,
        rim_exchange(grad_conv),
        cotangent,
        sea_mask,
        tap_rows(kernel[:, ::-1], row_count),
        layer_scale,
    )
    return (updated, grad_state, sum_in.T * grad_scale, sum_out * grad_scale)


def solution(mesh):
    return jax.shard_map(
        body,
        mesh=mesh,
        in_specs=(
            P("ch", None, "lon"),
            P(None, "lon"),
            P("ch", None),
            P("ch"),
            P(),
            P(),
            P(),
            P(),
            P(),
            P(),
            P("ch"),
            P("ch", None, "lon"),
        ),
        out_specs=(P("ch", None, "lon"), P("ch", None, "lon"), P(), P()),
        check_vma=False,
    )
```

time: 410 us -> 342 us (0.83); the launches traced: 403 us -> 342 us
  other arithmetic: 106 us -> 8.97 us
  Pallas kernels: 0 us -> 78.1 us
  matrix products: 51.3 us -> 0 us
  blocking collectives: 49.6 us -> 0 us
  waiting for transfers between devices: 124 us -> 153 us
  local copies, waits for them, and re-layouts: 37 us -> 63.8 us
    convert_element_type x6 -> x0, other arithmetic: 93.4 us -> none  [the longest x1 41 us: body(): (grad_out + depth_back(padded_grad, kernel, row_count, lon_cells)).astype...]
    pallas_call x0 -> x3, Pallas kernels: none -> 78.1 us  [the longest x1 38.2 us: block_math(): pl.pallas_call(functools.partial(math_kernel, hid_block), grid=(cells //...]
    dot_general x6 -> x0, matrix products: 51.3 us -> none  [the longest x1 14.4 us: block_math(): jnp.dot(weight_out, grad_cells, preferred_element_type=jnp.float32)]
    all_to_all x2 -> x0, blocking collectives: 49.6 us -> none  [the longest x1 25.3 us: body(): lax.all_to_all(conv_out, 'ch', split_axis=1, concat_axis=0, tiled=True)]
    all_to_all x2 -> x4, waiting for transfers between devices: 30.8 us -> 62.2 us  [the longest x2 33.8 us: body(): lax.all_to_all(cells.reshape(full_width, quarter, lon_cells), 'ch', split...]
    unnamed x65 -> x26, local copies, waits for them, and re-layouts: 16 us -> 22.8 us
    reshape x0 -> x5, local copies, waits for them, and re-layouts: none -> 6.73 us  [the longest x2 3.86 us: tap_rows(): return jnp.repeat(taps, row_count, axis=2)]
    pallas_call x0 -> x2, local copies, waits for them, and re-layouts: none -> 5.93 us  [body(): pl.pallas_call(functools.partial(forward_kernel, block), grid=(local_chan...]
  transfers between devices with their start and end apart: 7 -> 9, of which waited for: 3 -> 6; matrix products, arithmetic and copies ran while one was open for 20% -> 12% of each run, Pallas kernels for 0% -> 6%
where the time goes in v1:
time: 342 us
  waiting for transfers between devices  153 us (45%)
  Pallas kernels  78.1 us (23%)
  local copies, waits for them, and re-layouts  63.8 us (19%)
  starting transfers between devices  23.1 us (7%)
  between operations  14.3 us (4%)
  other arithmetic  8.97 us (3%)
    psum x1, waiting for transfers between devices, body(): sum_in, sum_out = lax.psum((part_in, part_out), ('lon', 'ch'))  88.7 us
    pallas_call x1, Pallas kernels, block_math(): pl.pallas_call(functools.partial(math_kernel, hid_block), grid=(cells //...  38.2 us
    all_to_all x2, waiting for transfers between devices, body(): lax.all_to_all(cells.reshape(full_width, quarter, lon_cells), 'ch', split...  33.8 us
    unnamed x26, local copies, waits for them, and re-layouts  22.8 us
    pallas_call x1, Pallas kernels, body(): pl.pallas_call(functools.partial(backward_kernel, block), grid=(local_cha...  20.4 us
    pallas_call x1, Pallas kernels, body(): pl.pallas_call(functools.partial(forward_kernel, block), grid=(local_chan...  19.5 us
    all_to_all x1, waiting for transfers between devices, body(): lax.all_to_all(conv_out, 'ch', split_axis=1, concat_axis=0, tiled=True)  19.2 us
    all_to_all x1, waiting for transfers between devices, body(): lax.all_to_all(grad_branch, 'ch', split_axis=1, concat_axis=0, tiled=True)  9.24 us
  transfers between devices with their start and end apart: 9, of which 6 were waited for; matrix products, arithmetic and copies ran while one was open for 12% of the time, Pallas kernels for 6%

profile of v1, /device:TPU:0, one launch (start us, length us, event | category | flops | bytes accessed | tf_op | source)
XLA Modules:
  0.0 341.6 jit_solution(2906078704815086852)
XLA Ops:
  7.2 2.7 fusion.1
  11.8 6.1 %collective-permute-start = (bf16[100,64,3]{0,1,2:T(8,128)(2,1)S(1)}, bf16[100,64,3]{0,1,2:T(8,128)(2,1)S(1)}, u32[]{:S(2)}, u32[]{:S(2)}) collective-permute-start(bf16[100,64,3]{0,1,2:T(8,128)(2,1)S(1)} %copy.62), channel_id=1, source_target_pairs={{4,0},{8,4},{12,8},{16,12},{20,16},{24,20},{28,24},{0,28},{5,1},{9... | collective-permute-start | bytes 115208 | tf_op jit(solution)/shard_map/ppermute | solution.py:30
  21.9 2.8 copy.40
  26.5 2.8 copy.41
  29.3 2.2 pad_maximum_fusion.rim
  31.5 19.5 %forward_conv.1 = (bf16[100,64,128]{2,1,0:T(8,128)(2,1)}, bf16[100,64,128]{2,1,0:T(8,128)(2,1)}) custom-call(bf16[100,64,128]{2,1,0:T(8,128)(2,1)} %state.3, bf16[100,64,128]{2,1,0:T(8,128)(2,1)} %pad_maximum_fusion.rim, bf16[100,64,128]{2,1,0:T(8,128)(2,1)} %cot.3, s32[64,128]{1,0:T(8,128)} %mask.3, f32[100,7,448]{2,1,0:T(8,128)} %copy.42.taps, f32[100]{0:T(128)} %bias.1, ...), custom_call_target="tpu_custom_call" | custom-call | tf_op jit(solution)/shard_map/forward_conv/pallas_call | solution.py:239
  51.0 3.7 %copy.43 = bf16[100,64,128]{2,0,1:T(8,128)(2,1)} copy(bf16[100,64,128]{2,1,0:T(8,128)(2,1)} %get-tuple-element.12) | data formatting | bytes 3276800 | tf_op jit(solution)/shard_map/forward_conv/pallas_call | solution.py:239
  54.7 3.7 %all-to-all-start = ((bf16[100,64,128]{2,0,1:T(8,128)(2,1)}), bf16[100,64,128]{2,0,1:T(8,128)(2,1)S(1)}, u32[]{:S(2)}, u32[]{:S(2)}) async-start(bf16[100,64,128]{2,0,1:T(8,128)(2,1)} %copy.43), calls=%async_computation | async-start | bytes 3407872 | tf_op jit(solution)/shard_map/all_to_all | solution.py:258
  58.4 2.2 copy.45
  60.7 19.2 %all-to-all-done = bf16[100,64,128]{2,0,1:T(8,128)(2,1)S(1)} async-done(((bf16[100,64,128]{2,0,1:T(8,128)(2,1)}), bf16[100,64,128]{2,0,1:T(8,128)(2,1)S(1)}, u32[]{:S(2)}, u32[]{:S(2)}) %all-to-all-start) | async-done | bytes 1638432 | tf_op jit(solution)/shard_map/all_to_all | solution.py:258
  79.8 3.8 %all-to-all-start.1 = ((bf16[100,64,128]{2,0,1:T(8,128)(2,1)}), bf16[100,64,128]{2,0,1:T(8,128)(2,1)S(1)}, u32[]{:S(2)}, u32[]{:S(2)}) async-start(bf16[100,64,128]{2,0,1:T(8,128)(2,1)} %copy.45), calls=%async_computation.1 | async-start | bytes 3407872 | tf_op jit(solution)/shard_map/all_to_all | solution.py:259
  83.6 3.4 %copy.47 = bf16[400,1600]{0,1:T(8,128)(2,1)} copy(bf16[400,1600]{1,0:T(8,128)(2,1)} %win.1) | data formatting | bytes 2560000 | tf_op args[6]
  87.1 3.5 %copy.51.wout = bf16[1600,400]{1,0:T(8,128)(2,1)} copy(bf16[1600,400]{0,1:T(8,128)(2,1)} %param.20) | data formatting | bytes 2560000 | tf_op args[8]
  95.6 9.2 %all-to-all-done.1 = bf16[100,64,128]{2,0,1:T(8,128)(2,1)S(1)} async-done(((bf16[100,64,128]{2,0,1:T(8,128)(2,1)}), bf16[100,64,128]{2,0,1:T(8,128)(2,1)S(1)}, u32[]{:S(2)}, u32[]{:S(2)}) %all-to-all-start.1) | async-done | bytes 1638432 | tf_op jit(solution)/shard_map/all_to_all | solution.py:259
  106.3 2.9 copy_bitcast_fusion
  109.2 38.2 %block_math.1 = (bf16[400,2048]{1,0:T(8,128)(2,1)}, bf16[400,2048]{1,0:T(8,128)(2,1)}, f32[1600,400]{1,0:T(8,128)}, f32[1600,400]{1,0:T(8,128)}) custom-call(bf16[400,2048]{1,0:T(8,128)(2,1)} %get-tuple-element.39.conv_cells, bf16[400,2048]{1,0:T(8,128)(2,1)} %get-tuple-element.38.grad_cells, f32[400,1]{1,0:T(8,128)} %copy.48.gain, f32[400,1]{1,0:T(8,128)} %copy.49.shift, ...), custom_call_target="tpu_custom_call" | custom-call | tf_op jit(solution)/shard_map/block_math/pallas_call | solution.py:174
  147.3 3.0 copy.67
  150.4 3.6 %all-to-all-start.3 = ((bf16[400,16,128]{2,1,0:T(8,128)(2,1)}), bf16[400,16,128]{2,1,0:T(8,128)(2,1)S(1)}, u32[]{:S(2)}, u32[]{:S(2)}) async-start(bf16[400,16,128]{2,1,0:T(8,128)(2,1)} %bitcast.30), calls=%async_computation.3 | async-start | bytes 3276800 | tf_op jit(solution)/shard_map/all_to_all | solution.py:273
  157.0 24.4 %all-to-all-done.3 = bf16[400,16,128]{2,1,0:T(8,128)(2,1)S(1)} async-done(((bf16[400,16,128]{2,1,0:T(8,128)(2,1)}), bf16[400,16,128]{2,1,0:T(8,128)(2,1)S(1)}, u32[]{:S(2)}, u32[]{:S(2)}) %all-to-all-start.3) | async-done | bytes 1638432 | tf_op jit(solution)/shard_map/all_to_all | solution.py:273
  181.5 3.6 %all-to-all-start.2 = ((bf16[400,16,128]{2,1,0:T(8,128)(2,1)}), bf16[400,16,128]{2,1,0:T(8,128)(2,1)S(1)}, u32[]{:S(2)}, u32[]{:S(2)}) async-start(bf16[400,16,128]{2,1,0:T(8,128)(2,1)} %bitcast.28), calls=%async_computation.2 | async-start | bytes 3276800 | tf_op jit(solution)/shard_map/all_to_all | solution.py:273
  187.4 2.9 copy.55
  194.7 1.9 copy.59.taps
  196.7 9.3 %all-to-all-done.2 = bf16[400,16,128]{2,1,0:T(8,128)(2,1)S(1)} async-done(((bf16[400,16,128]{2,1,0:T(8,128)(2,1)}), bf16[400,16,128]{2,1,0:T(8,128)(2,1)S(1)}, u32[]{:S(2)}, u32[]{:S(2)}) %all-to-all-start.2) | async-done | bytes 1638432 | tf_op jit(solution)/shard_map/all_to_all | solution.py:273
  207.7 2.8 copy.57
  210.5 2.8 copy.58
  213.3 2.2 pad_maximum_fusion.1.rim
  215.5 20.4 %backward_conv.1 = (bf16[100,64,128]{2,1,0:T(8,128)(2,1)}, bf16[100,64,128]{2,1,0:T(8,128)(2,1)}) custom-call(bf16[100,64,128]{2,1,0:T(8,128)(2,1)} %state.3, bf16[100,64,128]{2,1,0:T(8,128)(2,1)} %bitcast.41, bf16[100,64,128]{2,1,0:T(8,128)(2,1)} %bitcast.38, bf16[100,64,128]{2,1,0:T(8,128)(2,1)} %pad_maximum_fusion.1.rim, bf16[100,64,128]{2,1,0:T(8,128)(2,1)} %cot.3, ...), custom_call_target="tpu_custom_call" | custom-call | tf_op jit(solution)/shard_map/backward_conv/pallas_call | solution.py:282
  235.9 88.7 %all-reduce.3.cloned.1.call-done = (f32[1600,400]{1,0:T(8,128)}, f32[1600,400]{1,0:T(8,128)}) async-done(((f32[1600,400]{1,0:T(8,128)}, f32[1600,400]{1,0:T(8,128)}), (f32[1600,400]{1,0:T(8,128)}, f32[1600,400]{1,0:T(8,128)})) %all-reduce.3.cloned.1.call-update) | async-done | bytes 5120016 | tf_op jit(solution)/shard_map/psum | solution.py:271
  324.7 2.3 multiply_bitcast_fusion
  327.0 2.8 copy.60
  329.7 2.3 broadcast_multiply_fusion
  332.0 2.8 copy.61
  (48 shorter events, 25.7 us)
Async XLA Ops:
  9.9 9.9 %copy-start.4 = (f32[100,49]{0,1:T(8,128)S(1)}, f32[100,49]{0,1:T(8,128)}, u32[]{:S(2)}) copy-start(f32[100,49]{0,1:T(8,128)} %param.14) | copy-start | bytes 58804
  11.8 10.1 %collective-permute-start = (bf16[100,64,3]{0,1,2:T(8,128)(2,1)S(1)}, bf16[100,64,3]{0,1,2:T(8,128)(2,1)S(1)}, u32[]{:S(2)}, u32[]{:S(2)}) collective-permute-start(bf16[100,64,3]{0,1,2:T(8,128)(2,1)S(1)} %copy.62), channel_id=1, source_target_pairs={{4,0},{8,4},{12,8},{16,12},{20,16},{24,20},{28,24},{0,28},{5,1},{9... | collective-permute-start | bytes 115208 | tf_op jit(solution)/shard_map/ppermute | solution.py:30
  19.7 6.8 %collective-permute-start.1 = (bf16[100,64,3]{0,1,2:T(8,128)(2,1)S(1)}, bf16[100,64,3]{0,1,2:T(8,128)(2,1)S(1)}, u32[]{:S(2)}, u32[]{:S(2)}) collective-permute-start(bf16[100,64,3]{0,1,2:T(8,128)(2,1)S(1)} %copy.63), channel_id=1, source_target_pairs={{0,4},{4,8},{8,12},{12,16},{16,20},{20,24},{24,28},{28,0},{1,5},{5... | collective-permute-start | bytes 115208 | tf_op jit(solution)/shard_map/ppermute | solution.py:29
  54.7 3.7 %copy-start.3 = (bf16[100,64,128]{2,1,0:T(8,128)(2,1)S(1)}, bf16[100,64,128]{2,1,0:T(8,128)(2,1)}, u32[]{:S(2)}) copy-start(bf16[100,64,128]{2,1,0:T(8,128)(2,1)} %get-tuple-element.13) | copy-start | bytes 4915204
  54.7 25.2 %all-to-all-start = ((bf16[100,64,128]{2,0,1:T(8,128)(2,1)}), bf16[100,64,128]{2,0,1:T(8,128)(2,1)S(1)}, u32[]{:S(2)}, u32[]{:S(2)}) async-start(bf16[100,64,128]{2,0,1:T(8,128)(2,1)} %copy.43), calls=%async_computation | async-start | bytes 3407872 | tf_op jit(solution)/shard_map/all_to_all | solution.py:258
  79.8 25.0 %all-to-all-start.1 = ((bf16[100,64,128]{2,0,1:T(8,128)(2,1)}), bf16[100,64,128]{2,0,1:T(8,128)(2,1)S(1)}, u32[]{:S(2)}, u32[]{:S(2)}) async-start(bf16[100,64,128]{2,0,1:T(8,128)(2,1)} %copy.45), calls=%async_computation.1 | async-start | bytes 3407872 | tf_op jit(solution)/shard_map/all_to_all | solution.py:259
  87.1 3.5 %copy-start.5 = (f32[1600]{0:T(1024)S(1)}, f32[1600]{0:T(1024)}, u32[]{:S(2)}) copy-start(f32[1600]{0:T(1024)} %param.19) | copy-start | bytes 19204
  87.1 4.7 %copy-start.6 = (f32[400]{0:T(512)S(1)}, f32[400]{0:T(512)}, u32[]{:S(2)}) copy-start(f32[400]{0:T(512)} %param.16) | copy-start | bytes 4804
  87.1 5.6 %copy-start.7 = (f32[400]{0:T(512)S(1)}, f32[400]{0:T(512)}, u32[]{:S(2)}) copy-start(f32[400]{0:T(512)} %param.17) | copy-start | bytes 4804
  87.1 6.4 %copy-start.8 = (f32[400]{0:T(512)S(1)}, f32[400]{0:T(512)}, u32[]{:S(2)}) copy-start(f32[400]{0:T(512)} %param.21) | copy-start | bytes 4804
  104.9 1.4 copy-start.1
  150.4 31.1 %all-to-all-start.3 = ((bf16[400,16,128]{2,1,0:T(8,128)(2,1)}), bf16[400,16,128]{2,1,0:T(8,128)(2,1)S(1)}, u32[]{:S(2)}, u32[]{:S(2)}) async-start(bf16[400,16,128]{2,1,0:T(8,128)(2,1)} %bitcast.30), calls=%async_computation.3 | async-start | bytes 3276800 | tf_op jit(solution)/shard_map/all_to_all | solution.py:273
  153.9 170.7 %all-reduce.3.cloned.1.call-start = ((), (), s32[]{:S(2)}) async-start(), calls=%async_computation.4 | async-start | bytes 13107200 | tf_op jit(solution)/shard_map/psum | solution.py:271
  154.0 1.4 copy-start.2
  181.5 24.5 %all-to-all-start.2 = ((bf16[400,16,128]{2,1,0:T(8,128)(2,1)}), bf16[400,16,128]{2,1,0:T(8,128)(2,1)S(1)}, u32[]{:S(2)}, u32[]{:S(2)}) async-start(bf16[400,16,128]{2,1,0:T(8,128)(2,1)} %bitcast.28), calls=%async_computation.2 | async-start | bytes 3276800 | tf_op jit(solution)/shard_map/all_to_all | solution.py:273
  185.6 1.9 copy-start
  190.4 17.3 %collective-permute-start.2 = (bf16[100,64,3]{0,1,2:T(8,128)(2,1)S(1)}, bf16[100,64,3]{0,1,2:T(8,128)(2,1)S(1)}, u32[]{:S(2)}, u32[]{:S(2)}) collective-permute-start(bf16[100,64,3]{0,1,2:T(8,128)(2,1)S(1)} %copy.55), channel_id=1, source_target_pairs={{4,0},{8,4},{12,8},{16,12},{20,16},{24,20},{28,24},{0,28},{5,1},{9... | collective-permute-start | bytes 115208 | tf_op jit(solution)/shard_map/ppermute | solution.py:30
  193.9 16.6 %collective-permute-start.3 = (bf16[100,64,3]{0,1,2:T(8,128)(2,1)S(1)}, bf16[100,64,3]{0,1,2:T(8,128)(2,1)S(1)}, u32[]{:S(2)}, u32[]{:S(2)}) collective-permute-start(bf16[100,64,3]{0,1,2:T(8,128)(2,1)S(1)} %copy.56), channel_id=1, source_target_pairs={{0,4},{4,8},{8,12},{12,16},{16,20},{20,24},{24,28},{28,0},{1,5},{5... | collective-permute-start | bytes 115208 | tf_op jit(solution)/shard_map/ppermute | solution.py:29
Sparse Core Ops, SparseCore 0:
  160.7 163.9 all-reduce.2

commit v2 on v1

--- a/solution.py
+++ b/solution.py
@@ -68,18 +68,133 @@
     )
 
 
-def forward_kernel(block, state, rim, cot, mask, taps, bias, scale, conv_out, grad_branch):
-    first = pl.program_id(0) * block
+def greet_peers(peers):
+    me = lax.axis_index("ch")
+    barrier = pltpu.get_barrier_semaphore()
+    for r in range(1, peers):
+        pl.semaphore_signal(
+            barrier,
+            inc=1,
+            device_id={"ch": lax.rem(me + r, peers)},
+            device_id_type=pl.DeviceIdType.MESH,
+        )
+    pl.semaphore_wait(barrier, peers - 1)
+
+
+def forward_kernel(
+    block,
+    peers,
+    state,
+    rim,
+    cot,
+    mask,
+    taps,
+    bias,
+    scale,
+    conv_cells,
+    grad_cells,
+    conv_out,
+    grad_branch,
+    send_sem,
+    recv_sem,
+    own_sem,
+):
+    step = pl.program_id(0)
+    steps = pl.num_programs(0)
+    first = step * block
+    me = lax.axis_index("ch")
+    local_chan, row_count, _ = conv_out.shape
+    quarter = row_count // peers
+    pairs = ((conv_out, conv_cells), (grad_branch, grad_cells))
+
+    def views(which, at, target):
+        source, sink = pairs[which]
+        rows = pl.ds(pl.multiple_of(target * quarter, quarter), quarter)
+        return (
+            source.at[pl.ds(at * block, block), rows, :],
+            sink.at[pl.ds(me * local_chan + at * block, block)],
+        )
+
+    def remote(which, at, r):
+        target = lax.rem(me + r, peers)
+        source, sink = views(which, at, target)
+        return pltpu.make_async_remote_copy(
+            src_ref=source,
+            dst_ref=sink,
+            send_sem=send_sem.at[which, at, r - 1],
+            recv_sem=recv_sem.at[which, at, r - 1],
+            device_id={"ch": target},
+            device_id_type=pl.DeviceIdType.MESH,
+        )
+
+    def own(which, at):
+        source, sink = views(which, at, me)
+        return pltpu.make_async_copy(source, sink, own_sem.at[which, at])
+
+    @pl.when(step == 0)
+    def _():
+        greet_peers(peers)
+
     mask_f = mask[...].astype(jnp.float32)
 
     def channel(k, carry):
         conv = conv_channel(state[k], rim[k], taps[k])
-        conv_out[k] = (conv + bias[first + k]).astype(jnp.bfloat16)
+        conv_out[first + k] = (conv + bias[first + k]).astype(jnp.bfloat16)
         grad_out = cot[k].astype(jnp.float32) * mask_f
-        grad_branch[k] = (grad_out * scale[first + k]).astype(jnp.bfloat16)
+        grad_branch[first + k] = (grad_out * scale[first + k]).astype(jnp.bfloat16)
         return carry
 
     lax.fori_loop(0, block, channel, 0, unroll=2)
+    for which in range(2):
+        for r in range(1, peers):
+            remote(which, step, r).start()
+        own(which, step).start()
+
+    @pl.when(step == steps - 1)
+    def _():
+        def finish(at, carry):
+            for which in range(2):
+                for r in range(1, peers):
+                    remote(which, at, r).wait()
+                own(which, at).wait()
+            return carry
+
+        lax.fori_loop(0, steps, finish, 0)
+
+
+def return_kernel(
+    peers, branch_cells, grad_cells, branch, grad_conv, send_sem, recv_sem, own_sem
+):
+    me = lax.axis_index("ch")
+    local_chan, row_count, _ = branch.shape
+    quarter = row_count // peers
+    mine = pl.ds(pl.multiple_of(me * quarter, quarter), quarter)
+    greet_peers(peers)
+    copies = []
+    for which, (source, sink) in enumerate(((grad_cells, grad_conv), (branch_cells, branch))):
+        for r in range(1, peers):
+            target = lax.rem(me + r, peers)
+            copies.append(
+                pltpu.make_async_remote_copy(
+                    src_ref=source.at[pl.ds(target * local_chan, local_chan)],
+                    dst_ref=sink.at[:, mine, :],
+                    send_sem=send_sem.at[which, r - 1],
+                    recv_sem=recv_sem.at[which, r - 1],
+                    device_id={"ch": target},
+                    device_id_type=pl.DeviceIdType.MESH,
+                )
+            )
+        copies.append(
+            pltpu.make_async_copy(
+                source.at[pl.ds(me * local_chan, local_chan)],
+                sink.at[:, mine, :],
+                own_sem.at[which],
+            )
+        )
+    for copy in copies:
+        copy.start()
+    for copy in copies:
+        copy.wait()
 
 
 def backward_kernel(
@@ -113,10 +228,12 @@
     bias_out,
     branch,
     grad_conv,
+    in_total,
+    out_total,
+    act,
+    grad_pre,
     part_in,
     part_out,
-    act,
-    grad_pre,
 ):
     @pl.when(pl.program_id(0) == 0)
     def _():
@@ -161,6 +278,11 @@
         jnp.bfloat16
     )
 
+    @pl.when(pl.program_id(0) == pl.num_programs(0) - 1)
+    def _():
+        in_total[...] = part_in[...].astype(jnp.bfloat16)
+        out_total[...] = part_out[...].astype(jnp.bfloat16)
+
 
 def block_math(conv_cells, grad_cells, gain, shift, win, bias_in, wout, bias_out):
     full_width, cells = conv_cells.shape
@@ -170,7 +292,7 @@
     tile = pl.BlockSpec((full_width, block), lambda i: (0, i))
     whole = lambda shape: pl.BlockSpec(shape, lambda i: (0, 0))
     bf16 = jnp.bfloat16
-    part = jax.ShapeDtypeStruct((hid, full_width), jnp.float32)
+    part = jax.ShapeDtypeStruct((hid, full_width), bf16)
     return pl.pallas_call(
         functools.partial(math_kernel, hid_block),
         grid=(cells // block,),
@@ -193,7 +315,12 @@
             part,
             part,
         ],
-        scratch_shapes=[pltpu.VMEM((hid, block), bf16), pltpu.VMEM((hid, block), bf16)],
+        scratch_shapes=[
+            pltpu.VMEM((hid, block), bf16),
+            pltpu.VMEM((hid, block), bf16),
+            pltpu.VMEM((hid, full_width), jnp.float32),
+            pltpu.VMEM((hid, full_width), jnp.float32),
+        ],
         compiler_params=pltpu.CompilerParams(vmem_limit_bytes=VMEM_LIMIT),
         name="block_math",
     )(
@@ -236,13 +363,26 @@
     like = jax.ShapeDtypeStruct(ocean_state.shape, jnp.bfloat16)
     params = pltpu.CompilerParams(vmem_limit_bytes=VMEM_LIMIT)
 
-    conv_out, grad_branch = pl.pallas_call(
-        functools.partial(forward_kernel, block),
-        grid=(local_chan // block,),
+    quarter = row_count // chan_groups
+    steps = local_chan // block
+    shares = jax.ShapeDtypeStruct((full_width, quarter, lon_cells), jnp.bfloat16)
+    anywhere = pl.BlockSpec(memory_space=pl.ANY)
+    conv_cells, grad_cells = pl.pallas_call(
+        functools.partial(forward_kernel, block, chan_groups),
+        grid=(steps,),
         in_specs=[maps, maps, maps, one, rows, scalars, scalars],
-        out_specs=[maps, maps],
-        out_shape=[like, like],
-        compiler_params=params,
+        out_specs=[anywhere, anywhere],
+        out_shape=[shares, shares],
+        scratch_shapes=[
+            pltpu.VMEM(ocean_state.shape, jnp.bfloat16),
+            pltpu.VMEM(ocean_state.shape, jnp.bfloat16),
+            pltpu.SemaphoreType.DMA((2, steps, chan_groups - 1)),
+            pltpu.SemaphoreType.DMA((2, steps, chan_groups - 1)),
+            pltpu.SemaphoreType.DMA((2, steps)),
+        ],
+        compiler_params=pltpu.CompilerParams(
+            vmem_limit_bytes=VMEM_LIMIT, collective_id=0, has_side_effects=True
+        ),
         name="forward_conv",
     )(
         ocean_state,
@@ -253,11 +393,6 @@
         conv_bias,
         layer_scale,
     )
-    quarter = row_count // chan_groups
-    conv_cells, grad_cells = (
-        lax.all_to_all(conv_out, "ch", split_axis=1, concat_axis=0, tiled=True),
-        lax.all_to_all(grad_branch, "ch", split_axis=1, concat_axis=0, tiled=True),
-    )
     branch_cells, conv_grad_cells, part_in, part_out = block_math(
         conv_cells.reshape(full_width, quarter * lon_cells),
         grad_cells.reshape(full_width, quarter * lon_cells),
@@ -269,15 +404,22 @@
         bias_out,
     )
     sum_in, sum_out = lax.psum((part_in, part_out), ("lon", "ch"))
-    branch, grad_conv = (
-        lax.all_to_all(
-            cells.reshape(full_width, quarter, lon_cells),
-            "ch",
-            split_axis=0,
-            concat_axis=1,
-            tiled=True,
-        )
-        for cells in (branch_cells, conv_grad_cells)
+    branch, grad_conv = pl.pallas_call(
+        functools.partial(return_kernel, chan_groups),
+        in_specs=[anywhere, anywhere],
+        out_specs=[anywhere, anywhere],
+        out_shape=[like, like],
+        scratch_shapes=[
+            pltpu.SemaphoreType.DMA((2, chan_groups - 1)),
+            pltpu.SemaphoreType.DMA((2, chan_groups - 1)),
+            pltpu.SemaphoreType.DMA((2,)),
+        ],
+        compiler_params=pltpu.CompilerParams(collective_id=1, has_side_effects=True),
+        cost_estimate=pl.CostEstimate(flops=0, bytes_accessed=1, transcendentals=0),
+        name="return_cells",
+    )(
+        branch_cells.reshape(shares.shape),
+        conv_grad_cells.reshape(shares.shape),
     )
     updated, grad_state = pl.pallas_call(
         functools.partial(backward_kernel, block),
@@ -286,6 +428,7 @@
         out_specs=[maps, maps],
         out_shape=[like, like],
         compiler_params=params,
+        cost_estimate=pl.CostEstimate(flops=0, bytes_accessed=1, transcendentals=0),
         name="backward_conv",
     )(
         ocean_state,
@@ -297,7 +440,12 @@
         tap_rows(kernel[:, ::-1], row_count),
         layer_scale,
     )
-    return (updated, grad_state, sum_in.T * grad_scale, sum_out * grad_scale)
+    return (
+        updated,
+        grad_state,
+        sum_in.T.astype(jnp.float32) * grad_scale,
+        sum_out.astype(jnp.float32) * grad_scale,
+    )
 
 
 def solution(mesh):

time: 342 us -> 284 us (0.83)
  waiting for transfers between devices: 153 us -> 52.1 us
  Pallas kernels: 78.1 us -> 147 us
  local copies, waits for them, and re-layouts: 63.8 us -> 51.2 us
  starting transfers between devices: 23.1 us -> 10.9 us
    pallas_call x1 -> x2, Pallas kernels: 19.5 us -> 88.3 us  [the longest x1 46.3 us: body(): pl.pallas_call(functools.partial(return_kernel, chan_groups), in_specs=[a...]
    all_to_all x4 -> x0, waiting for transfers between devices: 62.2 us -> none  [the longest x2 33.8 us: body(): lax.all_to_all(cells.reshape(full_width, quarter, lon_cells), 'ch', split...]
    psum x1, waiting for transfers between devices: 88.7 us -> 49.6 us  [body(): sum_in, sum_out = lax.psum((part_in, part_out), ('lon', 'ch'))]
    all_to_all x4 -> x0, starting transfers between devices: 14.6 us -> none  [the longest x2 7.14 us: body(): lax.all_to_all(cells.reshape(full_width, quarter, lon_cells), 'ch', split...]
    pallas_call x2 -> x0, local copies, waits for them, and re-layouts: 5.93 us -> none  [body(): pl.pallas_call(functools.partial(forward_kernel, block), grid=(local_chan...]
    unnamed x26, local copies, waits for them, and re-layouts: 22.8 us -> 18.3 us
    all_to_all x4 -> x0, local copies, waits for them, and re-layouts: 3.78 us -> none  [the longest x2 2.18 us: body(): lax.all_to_all(cells.reshape(full_width, quarter, lon_cells), 'ch', split...]
  transfers between devices with their start and end apart: 9 -> 5, of which waited for: 6 -> 2; matrix products, arithmetic and copies ran while one was open for 12% -> 12% of each run, Pallas kernels for 6% -> 24%
where the time goes in v2:
time: 284 us; the launch traced here: 283 us
  Pallas kernels  147 us (52%)
  waiting for transfers between devices  52.1 us (18%)
  local copies, waits for them, and re-layouts  51.2 us (18%)
  between operations  14.3 us (5%)
  starting transfers between devices  10.9 us (4%)
  other arithmetic  8.11 us (3%)
    psum x1, waiting for transfers between devices, body(): sum_in, sum_out = lax.psum((part_in, part_out), ('lon', 'ch'))  49.6 us
    pallas_call x1, Pallas kernels, body(): pl.pallas_call(functools.partial(return_kernel, chan_groups), in_specs=[a...  46.3 us
    pallas_call x1, Pallas kernels, body(): pl.pallas_call(functools.partial(forward_kernel, block, chan_groups), gri...  42 us
    pallas_call x1, Pallas kernels, block_math(): pl.pallas_call(functools.partial(math_kernel, hid_block), grid=(cells //...  38.1 us
    pallas_call x1, Pallas kernels, body(): pl.pallas_call(functools.partial(backward_kernel, block), grid=(local_cha...  20.4 us
    unnamed x26, local copies, waits for them, and re-layouts  18.3 us
    ppermute x2, starting transfers between devices, rim_exchange(): lax.ppermute(head, 'lon', [((i + 1) % count, i) for i in range(count)])  10.6 us
    slice x3, local copies, waits for them, and re-layouts, rim_exchange(): head = cells[:, :, :RIM]  7.17 us
  transfers between devices with their start and end apart: 5, of which 2 were waited for; matrix products, arithmetic and copies ran while one was open for 12% of the time, Pallas kernels for 24%

profile of v2, /device:TPU:0, one launch (start us, length us, event | category | flops | bytes accessed | tf_op | source)
XLA Modules:
  0.0 283.4 jit_solution(3374322241221736737)
XLA Ops:
  7.2 2.6 fusion.1
  9.9 1.9 copy.50
  11.8 6.1 %collective-permute-start = (bf16[100,64,3]{0,1,2:T(8,128)(2,1)S(1)}, bf16[100,64,3]{0,1,2:T(8,128)(2,1)S(1)}, u32[]{:S(2)}, u32[]{:S(2)}) collective-permute-start(bf16[100,64,3]{0,1,2:T(8,128)(2,1)S(1)} %copy.50), channel_id=1, source_target_pairs={{4,0},{8,4},{12,8},{16,12},{20,16},{24,20},{28,24},{0,28},{5,1},{9... | collective-permute-start | bytes 115208 | tf_op jit(solution)/shard_map/ppermute | solution.py:30
  17.8 1.9 copy.51
  20.1 1.9 copy.36.taps
  22.0 2.2 copy.37
  24.2 2.2 copy.41.wout
  30.3 2.8 copy.34
  33.1 2.8 copy.35
  35.9 2.2 pad_maximum_fusion.rim
  38.1 42.0 %forward_conv.1 = (bf16[400,16,128]{2,1,0:T(8,128)(2,1)}, bf16[400,16,128]{2,1,0:T(8,128)(2,1)}) custom-call(bf16[100,64,128]{2,1,0:T(8,128)(2,1)} %state.3, bf16[100,64,128]{2,1,0:T(8,128)(2,1)} %pad_maximum_fusion.rim, bf16[100,64,128]{2,1,0:T(8,128)(2,1)} %cot.3, s32[64,128]{1,0:T(8,128)} %mask.3, f32[100,7,448]{2,1,0:T(8,128)} %copy.36.taps, f32[100]{0:T(128)} %bias.1, ...), custom_call_target="tpu_custom_call" | custom-call | tf_op jit(solution)/shard_map/forward_conv/pallas_call | solution.py:370
  80.1 4.8 %copy_bitcast_fusion = (bf16[400,2048]{1,0:T(8,128)(2,1)}, bf16[400,2048]{1,0:T(8,128)(2,1)}) fusion(bf16[50,8,16,128]{3,2,1,0:T(8,128)(2,1)} %bitcast.32, bf16[50,8,16,128]{3,2,1,0:T(8,128)(2,1)} %bitcast.31), kind=kLoop, calls=%fused_computation.2 | loop fusion | bytes 6553600 | tf_op jit(solution)/shard_map/reshape | solution.py:398
  84.8 38.1 %block_math.1 = (bf16[400,2048]{1,0:T(8,128)(2,1)}, bf16[400,2048]{1,0:T(8,128)(2,1)}, bf16[1600,400]{1,0:T(8,128)(2,1)}, bf16[1600,400]{1,0:T(8,128)(2,1)}) custom-call(bf16[400,2048]{1,0:T(8,128)(2,1)} %get-tuple-element.43.conv_cells, bf16[400,2048]{1,0:T(8,128)(2,1)} %get-tuple-element.42.grad_cells, f32[400,1]{1,0:T(8,128)} %copy.38.gain, ...), custom_call_target="tpu_custom_call" | custom-call | tf_op jit(solution)/shard_map/block_math/pallas_call | solution.py:296
  123.0 1.4 copy-done.3
  124.4 1.6 copy.54
  126.0 1.6 copy.55
  127.6 46.3 %return_cells.1 = (bf16[100,64,128]{2,1,0:T(8,128)(2,1)}, bf16[100,64,128]{2,1,0:T(8,128)(2,1)}) custom-call(bf16[400,16,128]{2,1,0:T(8,128)(2,1)} %bitcast.23, bf16[400,16,128]{2,1,0:T(8,128)(2,1)} %bitcast.24), custom_call_target="tpu_custom_call" | custom-call | bytes 1 | tf_op jit(solution)/shard_map/return_cells/pallas_call | solution.py:407
  173.9 2.7 fusion
  176.6 1.9 copy.43
  178.5 4.5 %collective-permute-start.2 = (bf16[100,64,3]{0,1,2:T(8,128)(2,1)S(1)}, bf16[100,64,3]{0,1,2:T(8,128)(2,1)S(1)}, u32[]{:S(2)}, u32[]{:S(2)}) collective-permute-start(bf16[100,64,3]{0,1,2:T(8,128)(2,1)S(1)} %copy.43), channel_id=1, source_target_pairs={{4,0},{8,4},{12,8},{16,12},{20,16},{24,20},{28,24},{0,28},{5,1},{9... | collective-permute-start | bytes 115208 | tf_op jit(solution)/shard_map/ppermute | solution.py:30
  183.0 1.9 copy.44
  185.1 1.9 copy.47.taps
  187.0 2.8 copy.45
  189.8 2.4 collective-permute-done.3
  192.2 2.8 copy.46
  195.0 2.2 pad_maximum_fusion.1.rim
  197.2 20.4 %backward_conv.1 = (bf16[100,64,128]{2,1,0:T(8,128)(2,1)}, bf16[100,64,128]{2,1,0:T(8,128)(2,1)}) custom-call(bf16[100,64,128]{2,1,0:T(8,128)(2,1)} %state.3, bf16[100,64,128]{2,1,0:T(8,128)(2,1)} %get-tuple-element.18.branch, bf16[100,64,128]{2,1,0:T(8,128)(2,1)} %get-tuple-element.19.grad_conv, bf16[100,64,128]{2,1,0:T(8,128)(2,1)} %pad_maximum_fusion.1.rim, ...), custom_call_target="tpu_custom_call" | custom-call | bytes 1 | tf_op jit(solution)/shard_map/backward_conv/pallas_call | solution.py:424
  217.6 49.6 %all-reduce.3.cloned.1.call-done = (bf16[1600,400]{1,0:T(8,128)(2,1)}, bf16[1600,400]{1,0:T(8,128)(2,1)}) async-done(((bf16[1600,400]{1,0:T(8,128)(2,1)}, bf16[1600,400]{1,0:T(8,128)(2,1)}), (bf16[1600,400]{1,0:T(8,128)(2,1)}, bf16[1600,400]{1,0:T(8,128)(2,1)})) %all-reduce.3.cloned.1.call-update) | async-done | bytes 2560016 | tf_op jit(solution)/shard_map/psum | solution.py:406
  267.3 1.9 multiply_bitcast_fusion
  269.2 2.8 copy.48
  271.9 1.9 convert_multiply_fusion
  273.8 2.8 copy.49
  (35 shorter events, 4.4 us)
Async XLA Ops:
  7.2 260.1 %all-reduce.3.cloned.1.call-start = ((), (), s32[]{:S(2)}) async-start(), calls=%async_computation | async-start | bytes 6553600 | tf_op jit(solution)/shard_map/psum | solution.py:406
  9.9 10.1 %copy-start.4 = (f32[100,49]{0,1:T(8,128)S(1)}, f32[100,49]{0,1:T(8,128)}, u32[]{:S(2)}) copy-start(f32[100,49]{0,1:T(8,128)} %param.14) | copy-start | bytes 58804
  11.8 18.5 %collective-permute-start = (bf16[100,64,3]{0,1,2:T(8,128)(2,1)S(1)}, bf16[100,64,3]{0,1,2:T(8,128)(2,1)S(1)}, u32[]{:S(2)}, u32[]{:S(2)}) collective-permute-start(bf16[100,64,3]{0,1,2:T(8,128)(2,1)S(1)} %copy.50), channel_id=1, source_target_pairs={{4,0},{8,4},{12,8},{16,12},{20,16},{24,20},{28,24},{0,28},{5,1},{9... | collective-permute-start | bytes 115208 | tf_op jit(solution)/shard_map/ppermute | solution.py:30
  19.7 13.4 %collective-permute-start.1 = (bf16[100,64,3]{0,1,2:T(8,128)(2,1)S(1)}, bf16[100,64,3]{0,1,2:T(8,128)(2,1)S(1)}, u32[]{:S(2)}, u32[]{:S(2)}) collective-permute-start(bf16[100,64,3]{0,1,2:T(8,128)(2,1)S(1)} %copy.51), channel_id=1, source_target_pairs={{0,4},{4,8},{8,12},{12,16},{16,20},{20,24},{24,28},{28,0},{1,5},{5... | collective-permute-start | bytes 115208 | tf_op jit(solution)/shard_map/ppermute | solution.py:29
  20.1 1.9 copy-start
  22.0 2.2 copy-start.1
  24.2 2.3 copy-start.5
  24.2 3.5 %copy-start.6 = (f32[400]{0:T(512)S(1)}, f32[400]{0:T(512)}, u32[]{:S(2)}) copy-start(f32[400]{0:T(512)} %param.16) | copy-start | bytes 4804
  24.2 4.3 %copy-start.7 = (f32[400]{0:T(512)S(1)}, f32[400]{0:T(512)}, u32[]{:S(2)}) copy-start(f32[400]{0:T(512)} %param.17) | copy-start | bytes 4804
  24.2 5.1 %copy-start.8 = (f32[400]{0:T(512)S(1)}, f32[400]{0:T(512)}, u32[]{:S(2)}) copy-start(f32[400]{0:T(512)} %param.21) | copy-start | bytes 4804
  123.0 1.4 copy-start.3
  124.4 1.6 copy-start.2
  178.5 8.5 %collective-permute-start.2 = (bf16[100,64,3]{0,1,2:T(8,128)(2,1)S(1)}, bf16[100,64,3]{0,1,2:T(8,128)(2,1)S(1)}, u32[]{:S(2)}, u32[]{:S(2)}) collective-permute-start(bf16[100,64,3]{0,1,2:T(8,128)(2,1)S(1)} %copy.43), channel_id=1, source_target_pairs={{4,0},{8,4},{12,8},{16,12},{20,16},{24,20},{28,24},{0,28},{5,1},{9... | collective-permute-start | bytes 115208 | tf_op jit(solution)/shard_map/ppermute | solution.py:30
  184.9 7.3 %collective-permute-start.3 = (bf16[100,64,3]{0,1,2:T(8,128)(2,1)S(1)}, bf16[100,64,3]{0,1,2:T(8,128)(2,1)S(1)}, u32[]{:S(2)}, u32[]{:S(2)}) collective-permute-start(bf16[100,64,3]{0,1,2:T(8,128)(2,1)S(1)} %copy.44), channel_id=1, source_target_pairs={{0,4},{4,8},{8,12},{12,16},{16,20},{20,24},{24,28},{28,0},{1,5},{5... | collective-permute-start | bytes 115208 | tf_op jit(solution)/shard_map/ppermute | solution.py:29
Sparse Core Ops, SparseCore 0:
  123.1 144.0 all-reduce.2

commit v3 on v2

--- a/solution.py
+++ b/solution.py
@@ -162,41 +162,6 @@
         lax.fori_loop(0, steps, finish, 0)
 
 
-def return_kernel(
-    peers, branch_cells, grad_cells, branch, grad_conv, send_sem, recv_sem, own_sem
-):
-    me = lax.axis_index("ch")
-    local_chan, row_count, _ = branch.shape
-    quarter = row_count // peers
-    mine = pl.ds(pl.multiple_of(me * quarter, quarter), quarter)
-    greet_peers(peers)
-    copies = []
-    for which, (source, sink) in enumerate(((grad_cells, grad_conv), (branch_cells, branch))):
-        for r in range(1, peers):
-            target = lax.rem(me + r, peers)
-            copies.append(
-                pltpu.make_async_remote_copy(
-                    src_ref=source.at[pl.ds(target * local_chan, local_chan)],
-                    dst_ref=sink.at[:, mine, :],
-                    send_sem=send_sem.at[which, r - 1],
-                    recv_sem=recv_sem.at[which, r - 1],
-                    device_id={"ch": target},
-                    device_id_type=pl.DeviceIdType.MESH,
-                )
-            )
-        copies.append(
-            pltpu.make_async_copy(
-                source.at[pl.ds(me * local_chan, local_chan)],
-                sink.at[:, mine, :],
-                own_sem.at[which],
-            )
-        )
-    for copy in copies:
-        copy.start()
-    for copy in copies:
-        copy.wait()
-
-
 def backward_kernel(
     block, state, branch, grad_conv, rim, cot, mask, taps, scale, updated, grad_state
 ):
@@ -216,6 +181,7 @@
 
 def math_kernel(
     hid_block,
+    peers,
     conv_cells,
     grad_cells,
     gain,
@@ -234,13 +200,61 @@
     grad_pre,
     part_in,
     part_out,
+    spread,
+    outgoing,
+    send_sem,
+    recv_sem,
+    own_sem,
 ):
-    @pl.when(pl.program_id(0) == 0)
+    step = pl.program_id(0)
+    steps = pl.num_programs(0)
+    me = lax.axis_index("ch")
+    full_width, block = conv_cells.shape
+    hid = win.shape[1]
+    local_chan = full_width // peers
+    padded = branch.shape[0]
+    sinks = (branch, grad_conv)
+
+    def views(which, at, target):
+        start = pl.multiple_of(me * (steps * block) + at * block, 128)
+        return (
+            outgoing.at[which, at, pl.ds(pl.multiple_of(target * padded, 16), padded), :],
+            sinks[which].at[:, pl.ds(start, block)],
+        )
+
+    def remote(which, at, r):
+        target = lax.rem(me + r, peers)
+        source, sink = views(which, at, target)
+        return pltpu.make_async_remote_copy(
+            src_ref=source,
+            dst_ref=sink,
+            send_sem=send_sem.at[which, at, r - 1],
+            recv_sem=recv_sem.at[which, at, r - 1],
+            device_id={"ch": target},
+            device_id_type=pl.DeviceIdType.MESH,
+        )
+
+    def own(which, at):
+        source, sink = views(which, at, me)
+        return pltpu.make_async_copy(source, sink, own_sem.at[which, at])
+
+    def send(which, cells):
+        for g in range(peers):
+            spread[g * padded : g * padded + local_chan, :] = cells[
+                g * local_chan : (g + 1) * local_chan, :
+            ]
+        outgoing[which, step] = spread[...].astype(jnp.bfloat16)
+        for r in range(1, peers):
+            remote(which, step, r).start()
+        own(which, step).start()
+
+    @pl.when(step == 0)
     def _():
+        greet_peers(peers)
         part_in[...] = jnp.zeros_like(part_in)
         part_out[...] = jnp.zeros_like(part_out)
-
-    full_width = conv_cells.shape[0]
+        spread[...] = jnp.zeros_like(spread)
+
     values = conv_cells[...].astype(jnp.float32)
     mean_val = jnp.sum(values, axis=0, keepdims=True) / full_width
     square = jnp.sum(values * values, axis=0, keepdims=True) / full_width
@@ -249,8 +263,8 @@
     normed = (centred * gain[...] + shift[...]).astype(jnp.bfloat16)
     grads = grad_cells[...]
     across = (((1,), (1,)), ((), ()))
-    for start in range(0, win_t.shape[0], hid_block):
-        here = slice(start, start + hid_block)
+    for start in range(0, hid, hid_block):
+        here = slice(start, min(start + hid_block, hid))
         v = jnp.dot(win_t[here, :], normed, preferred_element_type=jnp.float32) + bias_in[here, :]
         tangent = jnp.tanh(root_coef * (v + cubic_coef * v * v * v))
         act_h = (0.5 * v * (1.0 + tangent)).astype(jnp.bfloat16)
@@ -261,41 +275,51 @@
         grad_h = (grad_act * slope).astype(jnp.bfloat16)
         act[here, :] = act_h
         grad_pre[here, :] = grad_h
-        part_out[here, :] += lax.dot_general(
-            act_h, grads, across, preferred_element_type=jnp.float32
-        )
-        part_in[here, :] += lax.dot_general(
-            grad_h, normed, across, preferred_element_type=jnp.float32
-        )
-    branch[...] = (
-        jnp.dot(wout_t[...], act[...], preferred_element_type=jnp.float32) + bias_out[...]
-    ).astype(jnp.bfloat16)
+        part_out[:, here] += lax.dot_general(
+            grads, act_h, across, preferred_element_type=jnp.float32
+        )
+        part_in[:, here] += lax.dot_general(
+            normed, grad_h, across, preferred_element_type=jnp.float32
+        )
     grad_normed = jnp.dot(win[...], grad_pre[...], preferred_element_type=jnp.float32)
     scaled_grad = grad_normed * gain[...]
     mean_first = jnp.sum(scaled_grad, axis=0, keepdims=True) / full_width
     mean_second = jnp.sum(scaled_grad * centred, axis=0, keepdims=True) / full_width
-    grad_conv[...] = (inv_std * (scaled_grad - mean_first - centred * mean_second)).astype(
-        jnp.bfloat16
-    )
-
-    @pl.when(pl.program_id(0) == pl.num_programs(0) - 1)
+    send(1, inv_std * (scaled_grad - mean_first - centred * mean_second))
+    send(0, jnp.dot(wout_t[...], act[...], preferred_element_type=jnp.float32) + bias_out[...])
+
+    @pl.when(step == steps - 1)
     def _():
         in_total[...] = part_in[...].astype(jnp.bfloat16)
         out_total[...] = part_out[...].astype(jnp.bfloat16)
 
+        def finish(at, carry):
+            for which in range(2):
+                for r in range(1, peers):
+                    remote(which, at, r).wait()
+                own(which, at).wait()
+            return carry
+
+        lax.fori_loop(0, steps, finish, 0)
+
 
 def block_math(conv_cells, grad_cells, gain, shift, win, bias_in, wout, bias_out):
     full_width, cells = conv_cells.shape
     hid = win.shape[1]
+    peers = lax.axis_size("ch")
+    padded = -(-(full_width // peers) // 16) * 16
     block = largest_divisor(cells // 128, 2) * 128
-    hid_block = 16 * largest_divisor(hid // 16, 20)
+    steps = cells // block
+    hid_block = 5 * 128
     tile = pl.BlockSpec((full_width, block), lambda i: (0, i))
     whole = lambda shape: pl.BlockSpec(shape, lambda i: (0, 0))
+    anywhere = pl.BlockSpec(memory_space=pl.ANY)
     bf16 = jnp.bfloat16
-    part = jax.ShapeDtypeStruct((hid, full_width), bf16)
+    part = jax.ShapeDtypeStruct((full_width, hid), bf16)
+    back = jax.ShapeDtypeStruct((padded, peers * cells), bf16)
     return pl.pallas_call(
-        functools.partial(math_kernel, hid_block),
-        grid=(cells // block,),
+        functools.partial(math_kernel, hid_block, peers),
+        grid=(steps,),
         in_specs=[
             tile,
             tile,
@@ -308,20 +332,22 @@
             whole((full_width, hid)),
             whole((full_width, 1)),
         ],
-        out_specs=[tile, tile, whole((hid, full_width)), whole((hid, full_width))],
-        out_shape=[
-            jax.ShapeDtypeStruct((full_width, cells), bf16),
-            jax.ShapeDtypeStruct((full_width, cells), bf16),
-            part,
-            part,
-        ],
+        out_specs=[anywhere, anywhere, whole((full_width, hid)), whole((full_width, hid))],
+        out_shape=[back, back, part, part],
         scratch_shapes=[
             pltpu.VMEM((hid, block), bf16),
             pltpu.VMEM((hid, block), bf16),
-            pltpu.VMEM((hid, full_width), jnp.float32),
-            pltpu.VMEM((hid, full_width), jnp.float32),
+            pltpu.VMEM((full_width, hid), jnp.float32),
+            pltpu.VMEM((full_width, hid), jnp.float32),
+            pltpu.VMEM((peers * padded, block), jnp.float32),
+            pltpu.VMEM((2, steps, peers * padded, block), bf16),
+            pltpu.SemaphoreType.DMA((2, steps, peers - 1)),
+            pltpu.SemaphoreType.DMA((2, steps, peers - 1)),
+            pltpu.SemaphoreType.DMA((2, steps)),
         ],
-        compiler_params=pltpu.CompilerParams(vmem_limit_bytes=VMEM_LIMIT),
+        compiler_params=pltpu.CompilerParams(
+            vmem_limit_bytes=VMEM_LIMIT, collective_id=1, has_side_effects=True
+        ),
         name="block_math",
     )(
         conv_cells,
@@ -393,7 +419,7 @@
         conv_bias,
         layer_scale,
     )
-    branch_cells, conv_grad_cells, part_in, part_out = block_math(
+    branch, grad_conv, part_in, part_out = block_math(
         conv_cells.reshape(full_width, quarter * lon_cells),
         grad_cells.reshape(full_width, quarter * lon_cells),
         norm_gain,
@@ -404,22 +430,8 @@
         bias_out,
     )
     sum_in, sum_out = lax.psum((part_in, part_out), ("lon", "ch"))
-    branch, grad_conv = pl.pallas_call(
-        functools.partial(return_kernel, chan_groups),
-        in_specs=[anywhere, anywhere],
-        out_specs=[anywhere, anywhere],
-        out_shape=[like, like],
-        scratch_shapes=[
-            pltpu.SemaphoreType.DMA((2, chan_groups - 1)),
-            pltpu.SemaphoreType.DMA((2, chan_groups - 1)),
-            pltpu.SemaphoreType.DMA((2,)),
-        ],
-        compiler_params=pltpu.CompilerParams(collective_id=1, has_side_effects=True),
-        cost_estimate=pl.CostEstimate(flops=0, bytes_accessed=1, transcendentals=0),
-        name="return_cells",
-    )(
-        branch_cells.reshape(shares.shape),
-        conv_grad_cells.reshape(shares.shape),
+    branch, grad_conv = (
+        cells[:local_chan].reshape(ocean_state.shape) for cells in (branch, grad_conv)
     )
     updated, grad_state = pl.pallas_call(
         functools.partial(backward_kernel, block),
@@ -443,8 +455,8 @@
     return (
         updated,
         grad_state,
-        sum_in.T.astype(jnp.float32) * grad_scale,
-        sum_out.astype(jnp.float32) * grad_scale,
+        sum_in.astype(jnp.float32) * grad_scale,
+        sum_out.T.astype(jnp.float32) * grad_scale,
     )
 
 

time: 284 us -> 287 us (1.011)
  waiting for transfers between devices: 52.1 us -> 90.2 us
  Pallas kernels: 147 us -> 114 us
  local copies, waits for them, and re-layouts: 51.2 us -> 48.1 us
    psum x1, waiting for transfers between devices: 49.6 us -> 90.2 us  [body(): sum_in, sum_out = lax.psum((part_in, part_out), ('lon', 'ch'))]
    pallas_call x2 -> x1, Pallas kernels: 84.5 us -> 51.5 us  [block_math(): pl.pallas_call(functools.partial(math_kernel, hid_block, peers), grid=(st...]
    unnamed x26, local copies, waits for them, and re-layouts: 18.3 us -> 11.4 us
  transfers between devices with their start and end apart: 5 -> 5, of which waited for: 2 -> 1; matrix products, arithmetic and copies ran while one was open for 12% -> 13% of each run, Pallas kernels for 24% -> 7%
where the time goes in v3:
time: 287 us
  Pallas kernels  114 us (40%)
  waiting for transfers between devices  90.2 us (31%)
  local copies, waits for them, and re-layouts  48.1 us (17%)
  between operations  14.3 us (5%)
  starting transfers between devices  11.1 us (4%)
  other arithmetic  9.17 us (3%)
    psum x1, waiting for transfers between devices, body(): sum_in, sum_out = lax.psum((part_in, part_out), ('lon', 'ch'))  90.2 us
    pallas_call x1, Pallas kernels, block_math(): pl.pallas_call(functools.partial(math_kernel, hid_block, peers), grid=(st...  51.5 us
    pallas_call x1, Pallas kernels, body(): pl.pallas_call(functools.partial(forward_kernel, block, chan_groups), gri...  42 us
    pallas_call x1, Pallas kernels, body(): pl.pallas_call(functools.partial(backward_kernel, block), grid=(local_cha...  20.4 us
    unnamed x26, local copies, waits for them, and re-layouts  11.4 us
    ppermute x2, starting transfers between devices, rim_exchange(): lax.ppermute(head, 'lon', [((i + 1) % count, i) for i in range(count)])  10.8 us
    slice x3, local copies, waits for them, and re-layouts, rim_exchange(): head = cells[:, :, :RIM]  7.42 us
    ppermute x2, local copies, waits for them, and re-layouts, rim_exchange(): lax.ppermute(tail, 'lon', [(i, (i + 1) % count) for i in range(count)])  6.35 us
  transfers between devices with their start and end apart: 5, of which 1 were waited for; matrix products, arithmetic and copies ran while one was open for 13% of the time, Pallas kernels for 7%

profile of v3, /device:TPU:0, one launch (start us, length us, event | category | flops | bytes accessed | tf_op | source)
XLA Modules:
  0.0 286.9 jit_solution(13521256515076401573)
XLA Ops:
  7.2 2.6 fusion.1
  9.9 1.9 copy.44
  11.8 6.1 %collective-permute-start = (bf16[100,64,3]{0,1,2:T(8,128)(2,1)S(1)}, bf16[100,64,3]{0,1,2:T(8,128)(2,1)S(1)}, u32[]{:S(2)}, u32[]{:S(2)}) collective-permute-start(bf16[100,64,3]{0,1,2:T(8,128)(2,1)S(1)} %copy.44), channel_id=1, source_target_pairs={{4,0},{8,4},{12,8},{16,12},{20,16},{24,20},{28,24},{0,28},{5,1},{9... | collective-permute-start | bytes 115208 | tf_op jit(solution)/shard_map/ppermute | solution.py:30
  17.8 1.9 copy.45
  20.1 1.9 copy.32.taps
  22.0 2.2 copy.33
  24.2 2.2 copy.37.wout
  26.5 1.2 broadcast_in_dim.24.bias_in
  27.7 0.8 copy.34.gain
  28.5 0.8 copy.35.shift
  29.3 0.8 copy.38.bias_out
  30.2 2.8 copy.30
  33.0 2.8 copy.31
  35.9 2.2 pad_maximum_fusion.rim
  38.0 42.0 %forward_conv.1 = (bf16[400,16,128]{2,1,0:T(8,128)(2,1)}, bf16[400,16,128]{2,1,0:T(8,128)(2,1)}) custom-call(bf16[100,64,128]{2,1,0:T(8,128)(2,1)} %state.3, bf16[100,64,128]{2,1,0:T(8,128)(2,1)} %pad_maximum_fusion.rim, bf16[100,64,128]{2,1,0:T(8,128)(2,1)} %cot.3, s32[64,128]{1,0:T(8,128)} %mask.3, f32[100,7,448]{2,1,0:T(8,128)} %copy.32.taps, f32[100]{0:T(128)} %bias.1, ...), custom_call_target="tpu_custom_call" | custom-call | tf_op jit(solution)/shard_map/forward_conv/pallas_call | solution.py:396
  80.0 4.8 %copy_bitcast_fusion = (bf16[400,2048]{1,0:T(8,128)(2,1)}, bf16[400,2048]{1,0:T(8,128)(2,1)}) fusion(bf16[50,8,16,128]{3,2,1,0:T(8,128)(2,1)} %bitcast.35, bf16[50,8,16,128]{3,2,1,0:T(8,128)(2,1)} %bitcast.34), kind=kLoop, calls=%fused_computation.2 | loop fusion | bytes 6553600 | tf_op jit(solution)/shard_map/reshape | solution.py:424
  84.8 51.5 %block_math.1 = (bf16[112,8192]{1,0:T(8,128)(2,1)}, bf16[112,8192]{1,0:T(8,128)(2,1)}, bf16[400,1600]{1,0:T(8,128)(2,1)}, bf16[400,1600]{1,0:T(8,128)(2,1)}) custom-call(bf16[400,2048]{1,0:T(8,128)(2,1)} %get-tuple-element.27.conv_cells, bf16[400,2048]{1,0:T(8,128)(2,1)} %get-tuple-element.26.grad_cells, f32[400,1]{1,0:T(8,128)} %copy.34.gain, ...), custom_call_target="tpu_custom_call" | custom-call | tf_op jit(solution)/shard_map/block_math/pallas_call | solution.py:320
  136.3 1.5 copy-done.3
  138.4 1.9 fusion
  140.2 2.9 %copy.39 = bf16[100,64,3]{0,1,2:T(8,128)(2,1)S(1)} copy(bf16[100,64,3]{2,1,0:T(8,128)(2,1)} %get-tuple-element.22) | data formatting | bytes 76800 | tf_op jit(solution)/shard_map/slice | solution.py:27
  143.1 4.7 %collective-permute-start.2 = (bf16[100,64,3]{0,1,2:T(8,128)(2,1)S(1)}, bf16[100,64,3]{0,1,2:T(8,128)(2,1)S(1)}, u32[]{:S(2)}, u32[]{:S(2)}) collective-permute-start(bf16[100,64,3]{0,1,2:T(8,128)(2,1)S(1)} %copy.39), channel_id=1, source_target_pairs={{4,0},{8,4},{12,8},{16,12},{20,16},{24,20},{28,24},{0,28},{5,1},{9... | collective-permute-start | bytes 115208 | tf_op jit(solution)/shard_map/ppermute | solution.py:30
  147.9 1.9 copy.40
  150.0 2.0 copy.43.taps
  152.0 1.3 slice.27.grad_conv
  154.7 1.3 slice.26.branch
  156.0 2.8 copy.41
  158.8 3.5 %copy.42 = bf16[100,64,3]{2,1,0:T(8,128)(2,1)S(1)} copy(bf16[100,64,3]{0,1,2:T(8,128)(2,1)} %collective-permute-done.3) | data formatting | bytes 76800 | tf_op jit(solution)/shard_map/ppermute | solution.py:29
  162.3 2.2 pad_maximum_fusion.1.rim
  164.5 20.4 %backward_conv.1 = (bf16[100,64,128]{2,1,0:T(8,128)(2,1)}, bf16[100,64,128]{2,1,0:T(8,128)(2,1)}) custom-call(bf16[100,64,128]{2,1,0:T(8,128)(2,1)} %state.3, bf16[100,64,128]{2,1,0:T(8,128)(2,1)} %slice.26.branch, bf16[100,64,128]{2,1,0:T(8,128)(2,1)} %slice.27.grad_conv, bf16[100,64,128]{2,1,0:T(8,128)(2,1)} %pad_maximum_fusion.1.rim, ...), custom_call_target="tpu_custom_call" | custom-call | bytes 1 | tf_op jit(solution)/shard_map/backward_conv/pallas_call | solution.py:436
  185.0 90.2 %all-reduce.3.cloned.1.call-done = (bf16[400,1600]{1,0:T(8,128)(2,1)}, bf16[400,1600]{1,0:T(8,128)(2,1)}) async-done(((bf16[400,1600]{1,0:T(8,128)(2,1)}, bf16[400,1600]{1,0:T(8,128)(2,1)}), (bf16[400,1600]{1,0:T(8,128)(2,1)}, bf16[400,1600]{1,0:T(8,128)(2,1)})) %all-reduce.3.cloned.1.call-update) | async-done | bytes 2560016 | tf_op jit(solution)/shard_map/psum | solution.py:432
  275.2 3.1 %convert_multiply_fusion = f32[400,1600]{1,0:T(8,128)} fusion(bf16[400,1600]{1,0:T(8,128)(2,1)} %get-tuple-element.20), kind=kLoop, calls=%fused_computation.1 | loop fusion | flops 1280000 | bytes 3840000 | tf_op jit(solution)/shard_map/mul | solution.py:458
  278.3 1.7 multiply_bitcast_fusion
  (38 shorter events, 2.7 us)
Async XLA Ops:
  7.2 268.1 %all-reduce.3.cloned.1.call-start = ((), (), s32[]{:S(2)}) async-start(), calls=%async_computation | async-start | bytes 5324800 | tf_op jit(solution)/shard_map/psum | solution.py:432
  9.9 10.1 %copy-start.5 = (f32[100,49]{0,1:T(8,128)S(1)}, f32[100,49]{0,1:T(8,128)}, u32[]{:S(2)}) copy-start(f32[100,49]{0,1:T(8,128)} %param.14) | copy-start | bytes 58804
  11.8 18.5 %collective-permute-start = (bf16[100,64,3]{0,1,2:T(8,128)(2,1)S(1)}, bf16[100,64,3]{0,1,2:T(8,128)(2,1)S(1)}, u32[]{:S(2)}, u32[]{:S(2)}) collective-permute-start(bf16[100,64,3]{0,1,2:T(8,128)(2,1)S(1)} %copy.44), channel_id=1, source_target_pairs={{4,0},{8,4},{12,8},{16,12},{20,16},{24,20},{28,24},{0,28},{5,1},{9... | collective-permute-start | bytes 115208 | tf_op jit(solution)/shard_map/ppermute | solution.py:30
  19.7 13.3 %collective-permute-start.1 = (bf16[100,64,3]{0,1,2:T(8,128)(2,1)S(1)}, bf16[100,64,3]{0,1,2:T(8,128)(2,1)S(1)}, u32[]{:S(2)}, u32[]{:S(2)}) collective-permute-start(bf16[100,64,3]{0,1,2:T(8,128)(2,1)S(1)} %copy.45), channel_id=1, source_target_pairs={{0,4},{4,8},{8,12},{12,16},{16,20},{20,24},{24,28},{28,0},{1,5},{5... | collective-permute-start | bytes 115208 | tf_op jit(solution)/shard_map/ppermute | solution.py:29
  20.1 1.9 copy-start
  22.0 2.2 copy-start.1
  24.2 2.3 copy-start.6
  24.2 3.4 %copy-start.7 = (f32[400]{0:T(512)S(1)}, f32[400]{0:T(512)}, u32[]{:S(2)}) copy-start(f32[400]{0:T(512)} %param.16) | copy-start | bytes 4804
  24.2 4.3 %copy-start.8 = (f32[400]{0:T(512)S(1)}, f32[400]{0:T(512)}, u32[]{:S(2)}) copy-start(f32[400]{0:T(512)} %param.17) | copy-start | bytes 4804
  24.2 5.1 %copy-start.9 = (f32[400]{0:T(512)S(1)}, f32[400]{0:T(512)}, u32[]{:S(2)}) copy-start(f32[400]{0:T(512)} %param.21) | copy-start | bytes 4804
  136.3 1.5 copy-start.3
  143.1 12.8 %collective-permute-start.2 = (bf16[100,64,3]{0,1,2:T(8,128)(2,1)S(1)}, bf16[100,64,3]{0,1,2:T(8,128)(2,1)S(1)}, u32[]{:S(2)}, u32[]{:S(2)}) collective-permute-start(bf16[100,64,3]{0,1,2:T(8,128)(2,1)S(1)} %copy.39), channel_id=1, source_target_pairs={{4,0},{8,4},{12,8},{16,12},{20,16},{24,20},{28,24},{0,28},{5,1},{9... | collective-permute-start | bytes 115208 | tf_op jit(solution)/shard_map/ppermute | solution.py:30
  149.8 9.0 %collective-permute-start.3 = (bf16[100,64,3]{0,1,2:T(8,128)(2,1)S(1)}, bf16[100,64,3]{0,1,2:T(8,128)(2,1)}, u32[]{:S(2)}, u32[]{:S(2)}) collective-permute-start(bf16[100,64,3]{0,1,2:T(8,128)(2,1)S(1)} %copy.40), channel_id=1, source_target_pairs={{0,4},{4,8},{8,12},{12,16},{16,20},{20,24},{24,28},{28,0},{1,5},{5... | collective-permute-start | bytes 115208 | tf_op jit(solution)/shard_map/ppermute | solution.py:29
  152.0 2.1 copy-start.2
  275.2 3.1 %copy-start.4 = (bf16[400,1600]{1,0:T(8,128)(2,1)S(1)}, bf16[400,1600]{1,0:T(8,128)(2,1)}, u32[]{:S(2)}) copy-start(bf16[400,1600]{1,0:T(8,128)(2,1)} %get-tuple-element.21) | copy-start | bytes 3840004
Sparse Core Ops, SparseCore 0:
  136.4 138.7 all-reduce.2

commit v4 on v3

--- a/solution.py
+++ b/solution.py
@@ -275,11 +275,11 @@
         grad_h = (grad_act * slope).astype(jnp.bfloat16)
         act[here, :] = act_h
         grad_pre[here, :] = grad_h
-        part_out[:, here] += lax.dot_general(
-            grads, act_h, across, preferred_element_type=jnp.float32
-        )
-        part_in[:, here] += lax.dot_general(
-            normed, grad_h, across, preferred_element_type=jnp.float32
+        part_out[here, :] += lax.dot_general(
+            act_h, grads, across, preferred_element_type=jnp.float32
+        )
+        part_in[here, :] += lax.dot_general(
+            grad_h, normed, across, preferred_element_type=jnp.float32
         )
     grad_normed = jnp.dot(win[...], grad_pre[...], preferred_element_type=jnp.float32)
     scaled_grad = grad_normed * gain[...]
@@ -310,12 +310,12 @@
     padded = -(-(full_width // peers) // 16) * 16
     block = largest_divisor(cells // 128, 2) * 128
     steps = cells // block
-    hid_block = 5 * 128
+    hid_block = 16 * largest_divisor(hid // 16, 20)
     tile = pl.BlockSpec((full_width, block), lambda i: (0, i))
     whole = lambda shape: pl.BlockSpec(shape, lambda i: (0, 0))
     anywhere = pl.BlockSpec(memory_space=pl.ANY)
     bf16 = jnp.bfloat16
-    part = jax.ShapeDtypeStruct((full_width, hid), bf16)
+    part = jax.ShapeDtypeStruct((hid, full_width), bf16)
     back = jax.ShapeDtypeStruct((padded, peers * cells), bf16)
     return pl.pallas_call(
         functools.partial(math_kernel, hid_block, peers),
@@ -332,13 +332,13 @@
             whole((full_width, hid)),
             whole((full_width, 1)),
         ],
-        out_specs=[anywhere, anywhere, whole((full_width, hid)), whole((full_width, hid))],
+        out_specs=[anywhere, anywhere, whole((hid, full_width)), whole((hid, full_width))],
         out_shape=[back, back, part, part],
         scratch_shapes=[
             pltpu.VMEM((hid, block), bf16),
             pltpu.VMEM((hid, block), bf16),
-            pltpu.VMEM((full_width, hid), jnp.float32),
-            pltpu.VMEM((full_width, hid), jnp.float32),
+            pltpu.VMEM((hid, full_width), jnp.float32),
+            pltpu.VMEM((hid, full_width), jnp.float32),
             pltpu.VMEM((peers * padded, block), jnp.float32),
             pltpu.VMEM((2, steps, peers * padded, block), bf16),
             pltpu.SemaphoreType.DMA((2, steps, peers - 1)),
@@ -455,8 +455,8 @@
     return (
         updated,
         grad_state,
-        sum_in.astype(jnp.float32) * grad_scale,
-        sum_out.T.astype(jnp.float32) * grad_scale,
+        sum_in.T.astype(jnp.float32) * grad_scale,
+        sum_out.astype(jnp.float32) * grad_scale,
     )
 
 

time: 287 us -> 295 us (1.028)
  local copies, waits for them, and re-layouts: 48.1 us -> 53.7 us
    unnamed x26, local copies, waits for them, and re-layouts: 11.4 us -> 16.9 us
  transfers between devices with their start and end apart: 5 -> 5, of which waited for: 1 -> 1; matrix products, arithmetic and copies ran while one was open for 13% -> 12% of each run, Pallas kernels for 7% -> 7%
where the time goes in v4:
time: 295 us; the launch traced here: 294 us
  Pallas kernels  114 us (39%)
  waiting for transfers between devices  92.6 us (31%)
  local copies, waits for them, and re-layouts  53.7 us (18%)
  between operations  14.3 us (5%)
  starting transfers between devices  11.2 us (4%)
  other arithmetic  8.13 us (3%)
    psum x1, waiting for transfers between devices, body(): sum_in, sum_out = lax.psum((part_in, part_out), ('lon', 'ch'))  92.6 us
    pallas_call x1, Pallas kernels, block_math(): pl.pallas_call(functools.partial(math_kernel, hid_block, peers), grid=(st...  52 us
    pallas_call x1, Pallas kernels, body(): pl.pallas_call(functools.partial(forward_kernel, block, chan_groups), gri...  42 us
    pallas_call x1, Pallas kernels, body(): pl.pallas_call(functools.partial(backward_kernel, block), grid=(local_cha...  20.4 us
    unnamed x26, local copies, waits for them, and re-layouts  16.9 us
    ppermute x2, starting transfers between devices, rim_exchange(): lax.ppermute(head, 'lon', [((i + 1) % count, i) for i in range(count)])  10.8 us
    slice x3, local copies, waits for them, and re-layouts, rim_exchange(): head = cells[:, :, :RIM]  7.42 us
    ppermute x2, local copies, waits for them, and re-layouts, rim_exchange(): lax.ppermute(tail, 'lon', [(i, (i + 1) % count) for i in range(count)])  6.35 us
  transfers between devices with their start and end apart: 5, of which 1 were waited for; matrix products, arithmetic and copies ran while one was open for 12% of the time, Pallas kernels for 7%

profile of v4, /device:TPU:0, one launch (start us, length us, event | category | flops | bytes accessed | tf_op | source)
XLA Modules:
  0.0 294.3 jit_solution(17369526774159172671)
XLA Ops:
  7.2 2.6 fusion.1
  9.9 1.9 copy.50
  11.8 6.1 %collective-permute-start = (bf16[100,64,3]{0,1,2:T(8,128)(2,1)S(1)}, bf16[100,64,3]{0,1,2:T(8,128)(2,1)S(1)}, u32[]{:S(2)}, u32[]{:S(2)}) collective-permute-start(bf16[100,64,3]{0,1,2:T(8,128)(2,1)S(1)} %copy.50), channel_id=1, source_target_pairs={{4,0},{8,4},{12,8},{16,12},{20,16},{24,20},{28,24},{0,28},{5,1},{9... | collective-permute-start | bytes 115208 | tf_op jit(solution)/shard_map/ppermute | solution.py:30
  17.8 1.9 copy.51
  20.1 1.9 copy.36.taps
  22.0 2.2 copy.37
  24.2 2.2 copy.41.wout
  26.5 1.2 broadcast_in_dim.24.bias_in
  28.5 0.9 copy.39.shift
  30.3 2.8 copy.34
  33.1 2.8 copy.35
  35.9 2.2 pad_maximum_fusion.rim
  38.1 42.0 %forward_conv.1 = (bf16[400,16,128]{2,1,0:T(8,128)(2,1)}, bf16[400,16,128]{2,1,0:T(8,128)(2,1)}) custom-call(bf16[100,64,128]{2,1,0:T(8,128)(2,1)} %state.3, bf16[100,64,128]{2,1,0:T(8,128)(2,1)} %pad_maximum_fusion.rim, bf16[100,64,128]{2,1,0:T(8,128)(2,1)} %cot.3, s32[64,128]{1,0:T(8,128)} %mask.3, f32[100,7,448]{2,1,0:T(8,128)} %copy.36.taps, f32[100]{0:T(128)} %bias.1, ...), custom_call_target="tpu_custom_call" | custom-call | tf_op jit(solution)/shard_map/forward_conv/pallas_call | solution.py:396
  80.0 4.8 %copy_bitcast_fusion = (bf16[400,2048]{1,0:T(8,128)(2,1)}, bf16[400,2048]{1,0:T(8,128)(2,1)}) fusion(bf16[50,8,16,128]{3,2,1,0:T(8,128)(2,1)} %bitcast.35, bf16[50,8,16,128]{3,2,1,0:T(8,128)(2,1)} %bitcast.34), kind=kLoop, calls=%fused_computation.2 | loop fusion | bytes 6553600 | tf_op jit(solution)/shard_map/reshape | solution.py:424
  84.8 52.0 %block_math.1 = (bf16[112,8192]{1,0:T(8,128)(2,1)}, bf16[112,8192]{1,0:T(8,128)(2,1)}, bf16[1600,400]{1,0:T(8,128)(2,1)}, bf16[1600,400]{1,0:T(8,128)(2,1)}) custom-call(bf16[400,2048]{1,0:T(8,128)(2,1)} %get-tuple-element.39.conv_cells, bf16[400,2048]{1,0:T(8,128)(2,1)} %get-tuple-element.38.grad_cells, f32[400,1]{1,0:T(8,128)} %copy.38.gain, ...), custom_call_target="tpu_custom_call" | custom-call | tf_op jit(solution)/shard_map/block_math/pallas_call | solution.py:320
  136.9 1.5 copy-done.3
  138.9 1.9 fusion
  140.8 2.9 copy.43
  143.7 4.8 %collective-permute-start.2 = (bf16[100,64,3]{0,1,2:T(8,128)(2,1)S(1)}, bf16[100,64,3]{0,1,2:T(8,128)(2,1)S(1)}, u32[]{:S(2)}, u32[]{:S(2)}) collective-permute-start(bf16[100,64,3]{0,1,2:T(8,128)(2,1)S(1)} %copy.43), channel_id=1, source_target_pairs={{4,0},{8,4},{12,8},{16,12},{20,16},{24,20},{28,24},{0,28},{5,1},{9... | collective-permute-start | bytes 115208 | tf_op jit(solution)/shard_map/ppermute | solution.py:30
  148.5 1.9 copy.44
  150.5 2.0 copy.47.taps
  152.6 1.3 slice.27.grad_conv
  155.3 1.3 slice.26.branch
  156.6 2.8 copy.45
  159.4 3.5 %copy.46 = bf16[100,64,3]{2,1,0:T(8,128)(2,1)S(1)} copy(bf16[100,64,3]{0,1,2:T(8,128)(2,1)} %collective-permute-done.3) | data formatting | bytes 76800 | tf_op jit(solution)/shard_map/ppermute | solution.py:29
  162.9 2.2 pad_maximum_fusion.1.rim
  165.1 20.4 %backward_conv.1 = (bf16[100,64,128]{2,1,0:T(8,128)(2,1)}, bf16[100,64,128]{2,1,0:T(8,128)(2,1)}) custom-call(bf16[100,64,128]{2,1,0:T(8,128)(2,1)} %state.3, bf16[100,64,128]{2,1,0:T(8,128)(2,1)} %slice.26.branch, bf16[100,64,128]{2,1,0:T(8,128)(2,1)} %slice.27.grad_conv, bf16[100,64,128]{2,1,0:T(8,128)(2,1)} %pad_maximum_fusion.1.rim, ...), custom_call_target="tpu_custom_call" | custom-call | bytes 1 | tf_op jit(solution)/shard_map/backward_conv/pallas_call | solution.py:436
  185.6 92.6 %all-reduce.3.cloned.1.call-done = (bf16[1600,400]{1,0:T(8,128)(2,1)}, bf16[1600,400]{1,0:T(8,128)(2,1)}) async-done(((bf16[1600,400]{1,0:T(8,128)(2,1)}, bf16[1600,400]{1,0:T(8,128)(2,1)}), (bf16[1600,400]{1,0:T(8,128)(2,1)}, bf16[1600,400]{1,0:T(8,128)(2,1)})) %all-reduce.3.cloned.1.call-update) | async-done | bytes 2560016 | tf_op jit(solution)/shard_map/psum | solution.py:432
  278.2 1.9 multiply_bitcast_fusion
  280.0 2.8 copy.48
  282.8 1.9 convert_multiply_fusion
  284.7 2.8 copy.49
  (38 shorter events, 4.4 us)
Async XLA Ops:
  7.2 271.0 %all-reduce.3.cloned.1.call-start = ((), (), s32[]{:S(2)}) async-start(), calls=%async_computation | async-start | bytes 6553600 | tf_op jit(solution)/shard_map/psum | solution.py:432
  9.9 10.1 %copy-start.4 = (f32[100,49]{0,1:T(8,128)S(1)}, f32[100,49]{0,1:T(8,128)}, u32[]{:S(2)}) copy-start(f32[100,49]{0,1:T(8,128)} %param.14) | copy-start | bytes 58804
  11.8 18.5 %collective-permute-start = (bf16[100,64,3]{0,1,2:T(8,128)(2,1)S(1)}, bf16[100,64,3]{0,1,2:T(8,128)(2,1)S(1)}, u32[]{:S(2)}, u32[]{:S(2)}) collective-permute-start(bf16[100,64,3]{0,1,2:T(8,128)(2,1)S(1)} %copy.50), channel_id=1, source_target_pairs={{4,0},{8,4},{12,8},{16,12},{20,16},{24,20},{28,24},{0,28},{5,1},{9... | collective-permute-start | bytes 115208 | tf_op jit(solution)/shard_map/ppermute | solution.py:30
  19.7 13.4 %collective-permute-start.1 = (bf16[100,64,3]{0,1,2:T(8,128)(2,1)S(1)}, bf16[100,64,3]{0,1,2:T(8,128)(2,1)S(1)}, u32[]{:S(2)}, u32[]{:S(2)}) collective-permute-start(bf16[100,64,3]{0,1,2:T(8,128)(2,1)S(1)} %copy.51), channel_id=1, source_target_pairs={{0,4},{4,8},{8,12},{12,16},{16,20},{20,24},{24,28},{28,0},{1,5},{5... | collective-permute-start | bytes 115208 | tf_op jit(solution)/shard_map/ppermute | solution.py:29
  20.1 1.9 copy-start
  22.0 2.2 copy-start.1
  24.2 2.3 copy-start.5
  24.2 3.4 %copy-start.6 = (f32[400]{0:T(512)S(1)}, f32[400]{0:T(512)}, u32[]{:S(2)}) copy-start(f32[400]{0:T(512)} %param.16) | copy-start | bytes 4804
  24.2 4.2 %copy-start.7 = (f32[400]{0:T(512)S(1)}, f32[400]{0:T(512)}, u32[]{:S(2)}) copy-start(f32[400]{0:T(512)} %param.17) | copy-start | bytes 4804
  24.2 5.1 %copy-start.8 = (f32[400]{0:T(512)S(1)}, f32[400]{0:T(512)}, u32[]{:S(2)}) copy-start(f32[400]{0:T(512)} %param.21) | copy-start | bytes 4804
  136.8 1.5 copy-start.3
  143.7 12.9 %collective-permute-start.2 = (bf16[100,64,3]{0,1,2:T(8,128)(2,1)S(1)}, bf16[100,64,3]{0,1,2:T(8,128)(2,1)S(1)}, u32[]{:S(2)}, u32[]{:S(2)}) collective-permute-start(bf16[100,64,3]{0,1,2:T(8,128)(2,1)S(1)} %copy.43), channel_id=1, source_target_pairs={{4,0},{8,4},{12,8},{16,12},{20,16},{24,20},{28,24},{0,28},{5,1},{9... | collective-permute-start | bytes 115208 | tf_op jit(solution)/shard_map/ppermute | solution.py:30
  150.3 9.0 %collective-permute-start.3 = (bf16[100,64,3]{0,1,2:T(8,128)(2,1)S(1)}, bf16[100,64,3]{0,1,2:T(8,128)(2,1)}, u32[]{:S(2)}, u32[]{:S(2)}) collective-permute-start(bf16[100,64,3]{0,1,2:T(8,128)(2,1)S(1)} %copy.44), channel_id=1, source_target_pairs={{0,4},{4,8},{8,12},{12,16},{16,20},{20,24},{24,28},{28,0},{1,5},{5... | collective-permute-start | bytes 115208 | tf_op jit(solution)/shard_map/ppermute | solution.py:29
  152.6 2.1 copy-start.2
Sparse Core Ops, SparseCore 0:
  137.0 141.1 all-reduce.2
